TPU v7x, 256 devices: a whole 4x4x8 slice. The times are simulated.
256 devices in a mesh: grp: 4 (over z_hi), ta: 16 (over y, x), gz: 4 (over z_lo, core).
Axes of the slice: x: 4, y: 4, z: 8 (z_hi: 4, z_lo: 2; z = z_hi * 2 + z_lo), core: 2. Of those that a mesh axis runs over, the one named last changes fastest.
Arguments:
- source_field: float32 [2, 4, 3, 16, 32, 8, 128], P(None, None, None, 'grp', 'ta', 'gz'), may hold values from -6 to 6
- gauge_links: float32 [4, 2, 3, 3, 16, 32, 8, 8], P(None, None, None, None, 'grp', 'ta', 'gz'), may hold values from -2.5 to 2.5
- null_vectors: float32 [2, 4, 3, 16, 32, 8, 192], P(None, None, None, 'grp', 'ta', 'gz'), may hold values from -0.625 to 0.625
- coarse_links: float32 [5, 2, 24, 24, 4, 16, 4, 2], P(None, None, None, None, 'grp', 'ta', 'gz'), may hold values from -1 to 1
Outputs:
- solution_field: float32 [2, 4, 3, 16, 32, 8, 128], P(None, None, None, 'grp', 'ta', 'gz')
- coarse_solution: float32 [2, 24, 4, 4, 16, 4, 2], P(None, None, None, 'grp', 'ta', 'gz')
All inputs are finite; a program needn't handle non-finite values.
Results may differ from a plain program's by a relative error of at most 0.0003.
Values sent between devices are 32-bit elements; how exact they have to be, the bound alone decides.
A program may use at most 192 MiB of HBM per device.

v0:
```python
import functools

import jax
import jax.numpy as jnp
from jax import lax
from jax.experimental import pallas as pl
from jax.experimental.pallas import tpu as pltpu
from jax.sharding import PartitionSpec as P

MESH = pl.DeviceIdType.MESH
F32 = jnp.float32

site_mass = 2.0
hop_kappa = 0.1
fifth_hop = 0.4
wall_mass = 0.1
cheb_lower = 0.6
cheb_upper = 3.4
coarse_mass = 3.0
coarse_fifth = 0.3
basis_scale = 0.125
DEG = 4
CITERS = 4
gamma_table = (
    ((3, 0.0, 1.0), (2, 0.0, 1.0)),
    ((3, -1.0, 0.0), (2, 1.0, 0.0)),
    ((2, 0.0, 1.0), (3, 0.0, -1.0)),
    ((2, 1.0, 0.0), (3, 1.0, 0.0)),
)
AXES = ((0, "grp"), (2, "gz"), (3, "ta"))
COARSE_DIRS = (1, 3, 4)


def cheb_coefficients():
    centre = 0.5 * (cheb_upper + cheb_lower)
    half_width = 0.5 * (cheb_upper - cheb_lower)
    spread_ratio = centre / half_width
    ratio_now = 1.0 / spread_ratio
    pairs = []
    for _ in range(DEG - 1):
        ratio_next = 1.0 / (2.0 * spread_ratio - ratio_now)
        pairs.append((ratio_next * ratio_now, 2.0 * ratio_next / half_width))
        ratio_now = ratio_next
    return 1.0 / centre, pairs


START, PAIRS = cheb_coefficients()
ALPHA = [pair[0] for pair in PAIRS] + [0.0, 0.0] + [pair[0] for pair in PAIRS]
BETA = [pair[1] for pair in PAIRS] + [0.0, START] + [pair[1] for pair in PAIRS]


def plus(a, b, sign):
    return a + b if sign > 0 else a - b


def project(v, mu, f):
    real, imag = [], []
    for a in range(2):
        b, gr, gi = gamma_table[mu][a]
        if gr != 0.0:
            real.append(plus(v[0][a], v[0][b], f * gr))
            imag.append(plus(v[1][a], v[1][b], f * gr))
        else:
            real.append(plus(v[0][a], v[1][b], -f * gi))
            imag.append(plus(v[1][a], v[0][b], f * gi))
    return [real, imag]


def rebuild(acc, h, mu, f):
    for a in range(2):
        b, gr, gi = gamma_table[mu][a]
        acc[0][a] = acc[0][a] + h[0][a]
        acc[1][a] = acc[1][a] + h[1][a]
        if gr != 0.0:
            acc[0][b] = plus(acc[0][b], h[0][a], f * gr)
            acc[1][b] = plus(acc[1][b], h[1][a], f * gr)
        else:
            acc[0][b] = plus(acc[0][b], h[1][a], f * gi)
            acc[1][b] = plus(acc[1][b], h[0][a], -f * gi)


def link_mul(links, mu, t, h, dagger):
    out = [[None, None], [None, None]]
    for col in range(3):
        if dagger:
            lr, li = links[mu, 0, col, :, t], links[mu, 1, col, :, t]
        else:
            lr, li = links[mu, 0, :, col, t], links[mu, 1, :, col, t]
        for a in range(2):
            hr, hi = h[0][a][col][None], h[1][a][col][None]
            if dagger:
                re, im = lr * hr + li * hi, lr * hi - li * hr
            else:
                re, im = lr * hr - li * hi, lr * hi + li * hr
            out[0][a] = re if col == 0 else out[0][a] + re
            out[1][a] = im if col == 0 else out[1][a] + im
    return out


def each(fn, h):
    return [[fn(h[ri][a]) for a in range(2)] for ri in range(2)]


def dot(a, b, dims=((1,), (0,))):
    return lax.dot_general(
        a, b, (dims, ((), ())), precision=lax.Precision.HIGHEST, preferred_element_type=F32
    )


def iota(shape, dim):
    return lax.broadcasted_iota(jnp.int32, shape, dim)


def phases_of(sizes):
    phases = []
    for axis in ("gz", "ta", "grp"):
        size = sizes[axis]
        if size > 4 and size % 4 == 0:
            phases.append((axis, 1, 4))
            phases.append((axis, 4, size // 4))
        elif size > 1:
            phases.append((axis, 1, size))
    return phases


def kernel(sizes, src, gauge, null, coarse, u_out, e_out, p, r, u, acc, links, g8, hx, qx, hz, qz, ht, qt,
           sendx, sendz, sendt, recvx, recvz, recvt, nv, nvt, low, ff, fb, basis, crecv, ar_send, ar_recv,
           fsend, frecv, lsend, lrecv, csend, crsem, asend, arsem):
    me = {axis: lax.axis_index(axis) for axis in ("grp", "ta", "gz")}
    phases = phases_of(sizes)

    def moved(axis, by):
        return lax.rem(me[axis] + (by + sizes[axis]), sizes[axis])

    def in_group(axis, stride, count, by):
        own = lax.rem(lax.div(me[axis], stride), count)
        return me[axis] + (lax.rem(own + by, count) - own) * stride

    barrier = pltpu.get_barrier_semaphore()
    partners = []
    for _, axis in AXES:
        partners += [{axis: moved(axis, 1)}, {axis: moved(axis, -1)}]
    for axis, stride, count in phases:
        partners += [{axis: in_group(axis, stride, count, by)} for by in range(1, count)]
    for partner in partners:
        pl.semaphore_signal(barrier, inc=1, device_id=partner, device_id_type=MESH)

    for t in range(2):
        for x in range(4):
            rows = src[:, 4 * x + 2 * t:4 * x + 2 * t + 2, :].reshape(2, 4, 3, 2, 128)
            r[:, :, :, t, 2 * x:2 * x + 2, :] = rows
            p[:, :, :, t, 2 * x:2 * x + 2, :] = rows * START
            u[:, :, :, t, 2 * x:2 * x + 2, :] = rows * START
            g8[:, t, 2 * x:2 * x + 2, :] = gauge[:, 4 * x + 2 * t:4 * x + 2 * t + 2, :]
    spread_y = jnp.where((iota((8, 128), 1) & 7) == iota((8, 128), 0), 1.0, 0.0).astype(F32)
    tiled = dot(g8[...].reshape(72 * 16, 8), spread_y) * (-hop_kappa)
    links[...] = tiled.reshape(4, 2, 3, 3, 2, 8, 128)

    pl.semaphore_wait(barrier, len(partners))

    def low_copy(d):
        return pltpu.make_async_remote_copy(
            src_ref=coarse.at[pl.ds(COARSE_DIRS[d] * 96, 96)], dst_ref=low.at[d], send_sem=lsend.at[d],
            recv_sem=lrecv.at[d], device_id={AXES[d][1]: moved(AXES[d][1], 1)}, device_id_type=MESH)

    for d in range(3):
        low_copy(d).start()

    row8 = iota((8, 128), 0)
    lane8 = iota((8, 128), 1)

    def face_copy(d, side, slot):
        out, into = ((sendx, recvx), (sendz, recvz), (sendt, recvt))[d]
        axis = AXES[d][1]
        return pltpu.make_async_remote_copy(
            src_ref=out.at[side], dst_ref=into.at[slot, side], send_sem=fsend.at[2 * d + side],
            recv_sem=frecv.at[slot, 2 * d + side], device_id={axis: moved(axis, 2 * side - 1)},
            device_id_type=MESH)

    def field(ref, t):
        return [[ref[ri, s, :, t] for s in range(4)] for ri in range(2)]

    def build_null():
        for t in range(2):
            for x in range(4):
                nv[:, t, 2 * x:2 * x + 2, :] = null[:, x, t]

    def build_null_transposed():
        for ri in range(2):
            half = nv[12 * ri:12 * ri + 12].reshape(192, 192)
            nvt[192 * ri:192 * ri + 192, :] = half.T

    def build_coarse():
        for d in range(3):
            low_copy(d).wait()
        ff[...] = jnp.zeros_like(ff)
        fb[...] = jnp.zeros_like(fb)
        zero = jnp.zeros((24, 104), F32)

        def piece(ref, base, y):
            return jnp.concatenate([ref[pl.ds(base + y, 24, stride=2), :] * basis_scale, zero], axis=1)

        def placed(value, at):
            return value if at == 0 else pltpu.roll(value, at, 1)

        for y in range(2):
            blocks = []
            for direction in (0, 1, 3, 4, 2):
                blocks.append([piece(coarse, direction * 96 + ri * 48, y) for ri in range(2)])
            for ro in range(2):
                for tile in range(3):
                    total = None
                    for j in range(2):
                        if 2 * tile + j > 4:
                            continue
                        mr, mi = blocks[2 * tile + j]
                        first, second = (mr, -mi) if ro == 0 else (mi, mr)
                        part = placed(first, 64 * j) + placed(second, 64 * j + 32)
                        total = part if total is None else total + part
                    ff[64 * y + 32 * ro:64 * y + 32 * ro + 24, 128 * tile:128 * tile + 128] = total
        for block in range(4):
            parts = []
            for y in range(2):
                if block == 0:
                    parts.append([piece(coarse, 2 * 96 + ri * 48, 1 - y) for ri in range(2)])
                else:
                    parts.append([piece(low.at[block - 1], ri * 48, y) for ri in range(2)])
            for ri in range(2):
                total = None
                for y in range(2):
                    mr, mi = parts[y]
                    first, second = (mr, -mi) if ri == 0 else (mi, mr)
                    part = placed(first, 64 * y) + placed(second, 64 * y + 32)
                    total = part if total is None else total + part
                fb[64 * block + 32 * ri:64 * block + 32 * ri + 24, :] = total

    def apply_fine(k, hooks):
        slot = lax.rem(k, 2)
        even = (iota((3, 8, 128), 1) & 1) == 0
        for t in range(2):
            v = field(p, t)
            down = project(v, 0, -1.0)
            up = link_mul(links, 0, t, project(v, 0, 1.0), True)
            for ri in range(2):
                for a in range(2):
                    j = 2 * (2 * a + t)
                    sendx[0, 3 * ri:3 * ri + 3, j:j + 2, :] = down[ri][a][:, 0:2]
                    sendx[1, 3 * ri:3 * ri + 3, j:j + 2, :] = up[ri][a][:, 6:8]
                    hx[ri, a, :, t] = pltpu.roll(down[ri][a], 6, 1)
                    qx[ri, a, :, t] = pltpu.roll(up[ri][a], 2, 1)
        face_copy(0, 0, slot).start()
        face_copy(0, 1, slot).start()
        downs, ups = [], []
        for t in range(2):
            v = field(p, t)
            downs.append(project(v, 2, -1.0))
            ups.append(link_mul(links, 2, t, project(v, 2, 1.0), True))
        for ri in range(2):
            for a in range(2):
                for t in range(2):
                    hz[ri, a, :, t] = pltpu.roll(downs[t][ri][a], 7, 1)
                    qz[ri, a, :, t] = pltpu.roll(ups[t][ri][a], 1, 1)
                sendz[0, ri, a] = jnp.where(even, downs[0][ri][a], pltpu.roll(downs[1][ri][a], 1, 1))
                sendz[1, ri, a] = jnp.where(even, pltpu.roll(ups[0][ri][a], 7, 1), ups[1][ri][a])
        face_copy(1, 0, slot).start()
        face_copy(1, 1, slot).start()
        v = field(p, 0)
        down = project(v, 3, -1.0)
        own_up = link_mul(links, 3, 0, project(v, 3, 1.0), True)
        v = field(p, 1)
        own_down = project(v, 3, -1.0)
        up = link_mul(links, 3, 1, project(v, 3, 1.0), True)
        for ri in range(2):
            for a in range(2):
                sendt[0, ri, a] = down[ri][a]
                sendt[1, ri, a] = up[ri][a]
                ht[ri, a] = own_down[ri][a]
                qt[ri, a] = own_up[ri][a]
        face_copy(2, 0, slot).start()
        face_copy(2, 1, slot).start()

        lane = iota((3, 8, 128), 2)
        ypos = lane & 7
        below = jnp.where(lane < 8, fifth_hop * wall_mass, -fifth_hop).astype(F32)
        above = jnp.where(lane >= 120, fifth_hop * wall_mass, -fifth_hop).astype(F32)
        for t in range(2):
            v = field(p, t)
            total = [[None] * 4, [None] * 4]
            for ri in range(2):
                for s in range(4):
                    if s < 2:
                        side = below * pltpu.roll(v[ri][s], 8, 2)
                    else:
                        side = above * pltpu.roll(v[ri][s], 120, 2)
                    total[ri][s] = site_mass * v[ri][s] + side
            h = each(lambda w: jnp.where(ypos == 7, pltpu.roll(w, 7, 2), pltpu.roll(w, 127, 2)), project(v, 1, -1.0))
            rebuild(total, link_mul(links, 1, t, h, False), 1, -1.0)
            h = link_mul(links, 1, t, project(v, 1, 1.0), True)
            h = each(lambda w: jnp.where(ypos == 0, pltpu.roll(w, 121, 2), pltpu.roll(w, 1, 2)), h)
            rebuild(total, h, 1, 1.0)
            if t == 0:
                h = [[ht[ri, a] for a in range(2)] for ri in range(2)]
                rebuild(total, link_mul(links, 3, 0, h, False), 3, -1.0)
            else:
                rebuild(total, [[qt[ri, a] for a in range(2)] for ri in range(2)], 3, 1.0)
            for ri in range(2):
                for s in range(4):
                    acc[ri, s, :, t] = total[ri][s]
        for at, hook in hooks:
            pl.when(k == at)(hook)

        for d in (2, 0):
            face_copy(d, 0, slot).wait()
            face_copy(d, 1, slot).wait()
        for ri in range(2):
            for a in range(2):
                for t in range(2):
                    j = 2 * (2 * a + t)
                    hx[ri, a, :, t, 6:8, :] = recvx[slot, 0, 3 * ri:3 * ri + 3, j:j + 2, :]
                    qx[ri, a, :, t, 0:2, :] = recvx[slot, 1, 3 * ri:3 * ri + 3, j:j + 2, :]
        for t in range(2):
            total = field(acc, t)
            if t == 0:
                rebuild(total, [[recvt[slot, 1, ri, a] for a in range(2)] for ri in range(2)], 3, 1.0)
            else:
                h = [[recvt[slot, 0, ri, a] for a in range(2)] for ri in range(2)]
                rebuild(total, link_mul(links, 3, 1, h, False), 3, -1.0)
            h = [[hx[ri, a, :, t] for a in range(2)] for ri in range(2)]
            rebuild(total, link_mul(links, 0, t, h, False), 0, -1.0)
            rebuild(total, [[qx[ri, a, :, t] for a in range(2)] for ri in range(2)], 0, 1.0)
            for ri in range(2):
                for s in range(4):
                    acc[ri, s, :, t] = total[ri][s]
        face_copy(1, 0, slot).wait()
        face_copy(1, 1, slot).wait()
        alpha = jnp.float32(ALPHA[0])
        beta = jnp.float32(BETA[0])
        for at in range(1, 8):
            alpha = jnp.where(k == at, jnp.float32(ALPHA[at]), alpha)
            beta = jnp.where(k == at, jnp.float32(BETA[at]), beta)
        for t in range(2):
            total = field(acc, t)
            h = [[None, None], [None, None]]
            q = [[None, None], [None, None]]
            for ri in range(2):
                for a in range(2):
                    came, back = recvz[slot, 0, ri, a], recvz[slot, 1, ri, a]
                    if t == 0:
                        came = pltpu.roll(came, 1, 1)
                    else:
                        back = pltpu.roll(back, 7, 1)
                    h[ri][a] = jnp.where(even, hz[ri, a, :, t], came)
                    q[ri][a] = jnp.where(even, back, qz[ri, a, :, t])
            rebuild(total, link_mul(links, 2, t, h, False), 2, -1.0)
            rebuild(total, q, 2, 1.0)
            for ri in range(2):
                for s in range(4):
                    left = r[ri, s, :, t] - total[ri][s]
                    step = alpha * p[ri, s, :, t] + beta * left
                    r[ri, s, :, t] = left
                    p[ri, s, :, t] = step
                    u[ri, s, :, t] = u[ri, s, :, t] + step

    def first_half(k, carry):
        apply_fine(k, ((0, build_null), (1, build_null_transposed), (2, build_coarse)))
        return carry

    def second_half(k, carry):
        apply_fine(k, ())
        return carry

    lax.fori_loop(0, DEG, first_half, 0)

    diagonal = (iota((192, 256), 0) & 7) == (iota((192, 256), 1) & 7)
    selector = jnp.where(
        ((lane8 >> 5) == (row8 & 3)) & (((lane8 & 7) >> 2) == (row8 >> 2)), 1.0, 0.0).astype(F32)
    fold = jnp.where((iota((32, 192), 1) >> 3) == iota((32, 192), 0), 1.0, 0.0).astype(F32)
    both = jnp.concatenate([r[0].reshape(192, 128), r[1].reshape(192, 128)], axis=1)
    prod = dot(nvt[...], both)
    real = prod[0:192, 0:128] + prod[192:384, 128:256]
    imag = prod[0:192, 128:256] - prod[192:384, 0:128]
    kept = jnp.where(diagonal, jnp.concatenate([real, imag], axis=1), 0.0)
    summed = dot(fold, kept)
    stacked = jnp.concatenate([summed[:, 0:128], summed[:, 128:256]] * 2, axis=0)
    basis[0] = dot(selector, stacked, ((1,), (1,)))

    def coarse_copy(step, d, side):
        axis = AXES[d][1]
        return pltpu.make_async_remote_copy(
            src_ref=basis.at[step], dst_ref=crecv.at[step, 2 * d + side], send_sem=csend.at[step, 2 * d + side],
            recv_sem=crsem.at[step, 2 * d + side], device_id={axis: moved(axis, 2 * side - 1)},
            device_id_type=MESH)

    low_half = lane8 < 64
    for step in range(CITERS):
        for d in range(3):
            for side in range(2):
                coarse_copy(step, d, side).start()
        own = basis[step]
        other = pltpu.roll(own, 4, 0)
        layer = row8 & 3
        from_below = jnp.where(layer == 0, -wall_mass * pltpu.roll(own, 5, 0), pltpu.roll(own, 1, 0))
        from_above = jnp.where(layer == 3, -wall_mass * pltpu.roll(own, 3, 0), pltpu.roll(own, 7, 0))
        local = (-coarse_fifth * basis_scale) * (from_below + from_above)
        for d in range(3):
            for side in range(2):
                coarse_copy(step, d, side).wait()
        got = [crecv[step, j] for j in range(6)]
        ahead = jnp.concatenate(
            [jnp.where(low_half, own, got[0]), jnp.where(low_half, got[2], got[4]), other], axis=1)
        behind = jnp.concatenate(
            [jnp.where(low_half, other, got[1]), jnp.where(low_half, got[3], got[5])], axis=1)
        out = dot(ahead, ff[...], ((1,), (1,))) + dot(behind, fb[...])
        out = jnp.where((row8 < 4) == low_half, out, pltpu.roll(out, 64, 1))
        basis[step + 1] = out + local

    vectors = [basis[i] for i in range(CITERS + 1)]
    sign = jnp.where((lane8 & 32) == 0, 1.0, -1.0).astype(F32)
    turned = [sign * pltpu.roll(v, 32, 1) for v in vectors]
    entries = []
    for i in range(CITERS + 1):
        for j in range(i, CITERS + 1):
            entries.append((i, j, 0))
    for i in range(CITERS + 1):
        for j in range(i + 1, CITERS + 1):
            entries.append((i, j, 1))
    count = len(entries)
    products = jnp.concatenate(
        [jnp.where(low_half, vectors[i] * (vectors[j] if part == 0 else turned[j]), 0.0) for i, j, part in entries],
        axis=0)
    rowsum = dot(products, jnp.ones((128, 128), F32))
    mine = (iota((8 * count, 128), 0) >> 3) == iota((8 * count, 128), 1)
    sums = dot(jnp.ones((8, 8 * count), F32), jnp.where(mine, rowsum, 0.0))
    for number, (axis, stride, width) in enumerate(phases):
        ar_send[number] = sums
        copies = []
        for by in range(1, width):
            copies.append(pltpu.make_async_remote_copy(
                src_ref=ar_send.at[number], dst_ref=ar_recv.at[number, by - 1], send_sem=asend.at[number, by - 1],
                recv_sem=arsem.at[number, by - 1], device_id={axis: in_group(axis, stride, width, by)},
                device_id_type=MESH))
        for copy in copies:
            copy.start()
        for by, copy in enumerate(copies):
            copy.wait()
            sums = sums + ar_recv[number, by]

    size = CITERS + 1
    gram = [[None] * size for _ in range(size)]
    for number, (i, j, part) in enumerate(entries):
        value = jnp.broadcast_to(sums[:, number:number + 1], (8, 128))
        if part == 0:
            gram[i][j] = (value, None)
            if i != j:
                gram[j][i] = (value, None)
        else:
            gram[i][j] = (gram[i][j][0], value)
            gram[j][i] = (gram[j][i][0], -value)

    def gram_times(vector):
        result = []
        for i in range(size):
            tr, ti = None, None
            for j, (vr, vi) in enumerate(vector):
                gr, gi = gram[i][j]
                re, im = gr * vr, gr * vi
                if gi is not None:
                    re, im = re - gi * vi, im + gi * vr
                tr = re if tr is None else tr + re
                ti = im if ti is None else ti + im
            result.append((tr, ti))
        return result

    one, none = jnp.ones((8, 128), F32), jnp.zeros((8, 128), F32)
    coef = [(one, none)]
    seen = gram_times(coef)
    answer = [(none, none)] * CITERS
    grow = 1.0 / basis_scale
    for step in range(CITERS):
        image = []
        for i in range(step + 2):
            re = im = none
            if i <= step:
                re, im = coarse_mass * coef[i][0], coarse_mass * coef[i][1]
            if i >= 1:
                re, im = re + grow * coef[i - 1][0], im + grow * coef[i - 1][1]
            image.append((re, im))
        through = gram_times(image)
        top_r = top_i = bottom = none
        for i, (dr, di) in enumerate(image):
            top_r = top_r + (dr * seen[i][0] + di * seen[i][1])
            top_i = top_i + (dr * seen[i][1] - di * seen[i][0])
            bottom = bottom + (dr * through[i][0] + di * through[i][1])
        ar, ai = top_r / bottom, top_i / bottom
        for i, (cr, ci) in enumerate(coef):
            answer[i] = (answer[i][0] + (ar * cr - ai * ci), answer[i][1] + (ar * ci + ai * cr))
        padded = coef + [(none, none)]
        coef = [(cr - (ar * dr - ai * di), ci - (ar * di + ai * dr))
                for (cr, ci), (dr, di) in zip(padded, image)]
        seen = [(sr - (ar * zr - ai * zi), si - (ar * zi + ai * zr))
                for (sr, si), (zr, zi) in zip(seen, through)]
    found = none
    for i in range(CITERS):
        found = found + (answer[i][0] * vectors[i] - answer[i][1] * turned[i])
    e_out[...] = found

    spread = dot(found, selector, ((0,), (0,)))
    paired = jnp.concatenate([spread[0:32], spread[32:64]], axis=1)
    unfold = jnp.where((iota((192, 32), 0) >> 3) == iota((192, 32), 1), 1.0, 0.0).astype(F32)
    weights = jnp.where(diagonal, dot(unfold, paired), 0.0)
    prod = dot(nv[...].reshape(384, 192), weights)
    real = (prod[0:192, 0:128] - prod[192:384, 128:256]).reshape(4, 3, 2, 8, 128)
    imag = (prod[0:192, 128:256] + prod[192:384, 0:128]).reshape(4, 3, 2, 8, 128)
    p[0] = real
    p[1] = imag
    u[0] = u[0] + real
    u[1] = u[1] + imag

    lax.fori_loop(DEG, 2 * DEG, second_half, 0)
    for t in range(2):
        for x in range(4):
            u_out[:, 4 * x + 2 * t:4 * x + 2 * t + 2, :] = u[:, :, :, t, 2 * x:2 * x + 2, :].reshape(24, 2, 128)


def body(sizes, source_field, gauge_links, null_vectors, coarse_links):
    count = len(phases_of(sizes))
    vmem = pl.BlockSpec(memory_space=pltpu.VMEM)
    half = (2, 2, 3, 2, 8, 128)
    full = (2, 4, 3, 2, 8, 128)
    shapes = [full, full, full, full, (4, 2, 3, 3, 2, 8, 128), (72, 2, 8, 8), half, half, half, half,
              (2, 2, 3, 8, 128), (2, 2, 3, 8, 128),
              (2, 6, 8, 128), (2, 2, 2, 3, 8, 128), (2, 2, 2, 3, 8, 128),
              (2, 2, 6, 8, 128), (2, 2, 2, 2, 3, 8, 128), (2, 2, 2, 2, 3, 8, 128),
              (24, 2, 8, 192), (384, 192), (3, 96, 24), (128, 384), (256, 128), (CITERS + 1, 8, 128),
              (CITERS, 6, 8, 128), (count, 8, 128), (count, 3, 8, 128)]
    sems = [(6,), (2, 6), (3,), (3,), (CITERS, 6), (CITERS, 6), (count, 3), (count, 3)]
    out, found = pl.pallas_call(
        functools.partial(kernel, sizes),
        out_shape=(jax.ShapeDtypeStruct((24, 16, 128), F32), jax.ShapeDtypeStruct((8, 128), F32)),
        in_specs=[vmem] * 4,
        out_specs=(vmem, vmem),
        scratch_shapes=[pltpu.VMEM(shape, F32) for shape in shapes]
        + [pltpu.SemaphoreType.DMA(shape) for shape in sems],
        compiler_params=pltpu.CompilerParams(
            collective_id=0, has_side_effects=True, vmem_limit_bytes=40 * 1024 * 1024),
    )(
        source_field.reshape(24, 16, 128),
        gauge_links.reshape(72, 16, 8),
        null_vectors.reshape(24, 4, 2, 2, 192),
        coarse_links.transpose(0, 1, 2, 4, 5, 6, 7, 3).reshape(480, 24),
    )
    found = found[:, 0:64].reshape(2, 4, 2, 32)[:, :, :, 0:24].transpose(2, 3, 1, 0)
    return out.reshape(source_field.shape), found.reshape(2, 24, 4, 1, 1, 1, 2)


def solution(mesh):
    sizes = {axis: mesh.shape[axis] for axis in ("grp", "ta", "gz")}
    placed = (
        P(None, None, None, "grp", "ta", "gz", None),
        P(None, None, None, None, "grp", "ta", "gz", None),
        P(None, None, None, "grp", "ta", "gz", None),
        P(None, None, None, None, "grp", "ta", "gz", None),
    )
    return jax.shard_map(
        functools.partial(body, sizes),
        mesh=mesh,
        in_specs=placed,
        out_specs=(
            P(None, None, None, "grp", "ta", "gz", None),
            P(None, None, None, "grp", "ta", "gz", None),
        ),
        check_vma=False,
    )
```

profile of v0, /device:TPU:1, one launch (start us, length us, event | category | flops | bytes accessed | tf_op | source)
XLA Modules:
  0.0 95.6 jit_solution(5983254336038819066)
XLA Ops:
  0.6 0.0 copy-start
  0.6 1.1 %copy-done = f32[4,2,3,3,4,2,2,8]{7,6,5,4,3,2,1,0:T(2,128)S(1)} copy-done((f32[4,2,3,3,4,2,2,8]{7,6,5,4,3,2,1,0:T(2,128)S(1)}, f32[4,2,3,3,4,2,2,8]{7,6,5,4,3,2,1,0:T(2,128)}, u32[]{:S(2)}) %copy-start) | copy-done | bytes 36888
  1.7 0.0 copy-start.1
  1.7 1.0 %copy-done.1 = f32[2,4,3,4,2,2,192]{6,5,4,3,2,1,0:T(2,128)S(1)} copy-done((f32[2,4,3,4,2,2,192]{6,5,4,3,2,1,0:T(2,128)S(1)}, f32[2,4,3,4,2,2,192]{6,5,4,3,2,1,0:T(2,128)}, u32[]{:S(2)}) %copy-start.1) | copy-done | bytes 294936
  2.7 0.0 copy-start.2
  2.7 0.9 copy-done.2
  3.6 0.0 copy-start.3
  3.6 0.9 copy-done.3
  4.6 89.6 %shard_map.59 = (f32[24,16,128]{2,1,0:T(8,128)S(1)}, f32[8,128]{1,0:T(8,128)S(1)}) custom-call(f32[24,16,128]{2,1,0:T(8,128)S(1)} %bitcast.18, f32[72,16,8]{2,1,0:T(8,128)S(1)} %bitcast.14, f32[24,4,2,2,192]{4,3,2,1,0:T(2,128)S(1)} %bitcast.15, f32[480,24]{1,0:T(8,128)S(1)} %bitcast.16), custom_call_target="tpu_custom_call" | custom-call | tf_op jit(solution)/shard_map/pallas_call | solution.py:537
  94.2 0.1 reshape.30
  94.3 0.6 copy.9
  94.9 0.7 copy.11
Async XLA Ops:
  0.6 1.1 %copy-start = (f32[4,2,3,3,4,2,2,8]{7,6,5,4,3,2,1,0:T(2,128)S(1)}, f32[4,2,3,3,4,2,2,8]{7,6,5,4,3,2,1,0:T(2,128)}, u32[]{:S(2)}) copy-start(f32[4,2,3,3,4,2,2,8]{7,6,5,4,3,2,1,0:T(2,128)} %param.5) | copy-start | bytes 110596
  1.7 1.0 %copy-start.1 = (f32[2,4,3,4,2,2,192]{6,5,4,3,2,1,0:T(2,128)S(1)}, f32[2,4,3,4,2,2,192]{6,5,4,3,2,1,0:T(2,128)}, u32[]{:S(2)}) copy-start(f32[2,4,3,4,2,2,192]{6,5,4,3,2,1,0:T(2,128)} %param.6) | copy-start | bytes 884740
  2.7 0.9 copy-start.2
  3.6 0.9 copy-start.3
where the time goes:
time: 95.8 us; the launch traced here: 95.6 us
  Pallas kernels  89.6 us (94%)
  local copies, waits for them, and re-layouts  5.28 us (6%)
    pallas_call x1, Pallas kernels, body(): pl.pallas_call(functools.partial(kernel, sizes), out_shape=(jax.ShapeDtyp...  89.6 us
    unnamed x10, local copies, waits for them, and re-layouts  5.2 us

commit v1 on v0

v1 whole, which is shorter than its diff:
```python
import functools

import jax
import jax.numpy as jnp
from jax import lax
from jax.experimental import pallas as pl
from jax.experimental.pallas import tpu as pltpu
from jax.sharding import PartitionSpec as P

MESH = pl.DeviceIdType.MESH
F32 = jnp.float32

site_mass = 2.0
hop_kappa = 0.1
fifth_hop = 0.4
wall_mass = 0.1
cheb_lower = 0.6
cheb_upper = 3.4
coarse_mass = 3.0
coarse_fifth = 0.3
basis_scale = 0.125
DEG = 4
CITERS = 4
gamma_table = (
    ((3, 0.0, 1.0), (2, 0.0, 1.0)),
    ((3, -1.0, 0.0), (2, 1.0, 0.0)),
    ((2, 0.0, 1.0), (3, 0.0, -1.0)),
    ((2, 1.0, 0.0), (3, 1.0, 0.0)),
)
AXES = ((0, "grp"), (2, "gz"), (3, "ta"))
COARSE_DIRS = (1, 3, 4)


def cheb_coefficients():
    centre = 0.5 * (cheb_upper + cheb_lower)
    half_width = 0.5 * (cheb_upper - cheb_lower)
    spread_ratio = centre / half_width
    ratio_now = 1.0 / spread_ratio
    pairs = []
    for _ in range(DEG - 1):
        ratio_next = 1.0 / (2.0 * spread_ratio - ratio_now)
        pairs.append((ratio_next * ratio_now, 2.0 * ratio_next / half_width))
        ratio_now = ratio_next
    return 1.0 / centre, pairs


START, PAIRS = cheb_coefficients()
ALPHA = [pair[0] for pair in PAIRS] + [0.0, 0.0] + [pair[0] for pair in PAIRS]
BETA = [pair[1] for pair in PAIRS] + [0.0, START] + [pair[1] for pair in PAIRS]


def plus(a, b, sign):
    return a + b if sign > 0 else a - b


def project(v, mu, f):
    real, imag = [], []
    for a in range(2):
        b, gr, gi = gamma_table[mu][a]
        if gr != 0.0:
            real.append(plus(v[0][a], v[0][b], f * gr))
            imag.append(plus(v[1][a], v[1][b], f * gr))
        else:
            real.append(plus(v[0][a], v[1][b], -f * gi))
            imag.append(plus(v[1][a], v[0][b], f * gi))
    return [real, imag]


def rebuild(acc, h, mu, f):
    for a in range(2):
        b, gr, gi = gamma_table[mu][a]
        acc[0][a] = acc[0][a] + h[0][a]
        acc[1][a] = acc[1][a] + h[1][a]
        if gr != 0.0:
            acc[0][b] = plus(acc[0][b], h[0][a], f * gr)
            acc[1][b] = plus(acc[1][b], h[1][a], f * gr)
        else:
            acc[0][b] = plus(acc[0][b], h[1][a], f * gi)
            acc[1][b] = plus(acc[1][b], h[0][a], -f * gi)


def link_mul(links, mu, t, h, dagger):
    out = [[None, None], [None, None]]
    for col in range(3):
        if dagger:
            lr, li = links[mu, 0, col, :, t], links[mu, 1, col, :, t]
        else:
            lr, li = links[mu, 0, :, col, t], links[mu, 1, :, col, t]
        for a in range(2):
            hr, hi = h[0][a][col][None], h[1][a][col][None]
            if dagger:
                re, im = lr * hr + li * hi, lr * hi - li * hr
            else:
                re, im = lr * hr - li * hi, lr * hi + li * hr
            out[0][a] = re if col == 0 else out[0][a] + re
            out[1][a] = im if col == 0 else out[1][a] + im
    return out


def each(fn, h):
    return [[fn(h[ri][a]) for a in range(2)] for ri in range(2)]


def dot(a, b, dims=((1,), (0,))):
    return lax.dot_general(
        a, b, (dims, ((), ())), precision=lax.Precision.HIGHEST, preferred_element_type=F32
    )


def iota(shape, dim):
    return lax.broadcasted_iota(jnp.int32, shape, dim)


def kernel(sizes, src_in, gauge_in, null_in, coarse_in, u_out, e_out, src, gauge, null, coarse, p, u, fields, acc, links, g8,
           hx, qx, hz, qz, ht, qt, sendx, sendz, sendt, recvx, recvz, recvt, nv, nvt, low, ff, fb, basis, crecv, ar_send,
           ar_recv, isem, fsend, frecv, lsend, lrecv, csend, crsem, asend, arsem):
    me = {axis: lax.axis_index(axis) for axis in ("grp", "ta", "gz")}
    plane = sizes["grp"] * sizes["gz"]
    spot = me["grp"] * sizes["gz"] + me["gz"]

    def moved(axis, by):
        return lax.rem(me[axis] + (by + sizes[axis]), sizes[axis])

    def in_plane(by):
        other = lax.rem(spot + by, plane)
        return {"grp": lax.div(other, sizes["gz"]), "gz": lax.rem(other, sizes["gz"])}

    groups = ([{"ta": moved("ta", by)} for by in range(1, sizes["ta"])], [in_plane(by) for by in range(1, plane)])

    barrier = pltpu.get_barrier_semaphore()
    for partner in groups[0] + groups[1]:
        pl.semaphore_signal(barrier, inc=1, device_id=partner, device_id_type=MESH)

    loads = [pltpu.make_async_copy(a, b, isem.at[i]) for i, (a, b) in enumerate(
        ((gauge_in, gauge), (src_in, src), (coarse_in, coarse), (null_in, null)))]
    for load in loads:
        load.start()

    r = fields.at[4]

    loads[0].wait()
    for t in range(2):
        for x in range(4):
            g8[:, t, 2 * x:2 * x + 2, :] = gauge[:, 4 * x + 2 * t:4 * x + 2 * t + 2, :]
    spread_y = jnp.where((iota((8, 128), 1) & 7) == iota((8, 128), 0), 1.0, 0.0).astype(F32)
    tiled = dot(g8[...].reshape(72 * 16, 8), spread_y) * (-hop_kappa)
    links[...] = tiled.reshape(4, 2, 3, 3, 2, 8, 128)
    loads[1].wait()
    for t in range(2):
        for x in range(4):
            rows = src[:, 4 * x + 2 * t:4 * x + 2 * t + 2, :].reshape(2, 4, 3, 2, 128)
            r[:, :, :, t, 2 * x:2 * x + 2, :] = rows
            p[:, :, :, t, 2 * x:2 * x + 2, :] = rows * START
            u[:, :, :, t, 2 * x:2 * x + 2, :] = rows * START
    loads[2].wait()

    pl.semaphore_wait(barrier, len(groups[0]) + len(groups[1]))

    def low_copy(d):
        return pltpu.make_async_remote_copy(
            src_ref=coarse.at[pl.ds(COARSE_DIRS[d] * 96, 96)], dst_ref=low.at[d], send_sem=lsend.at[d],
            recv_sem=lrecv.at[d], device_id={AXES[d][1]: moved(AXES[d][1], 1)}, device_id_type=MESH)

    row8 = iota((8, 128), 0)
    lane8 = iota((8, 128), 1)

    def face_copy(d, side, ls, rs):
        out, into = ((sendx, recvx), (sendz, recvz), (sendt, recvt))[d]
        axis = AXES[d][1]
        return pltpu.make_async_remote_copy(
            src_ref=out.at[ls, side], dst_ref=into.at[rs, side], send_sem=fsend.at[ls, 2 * d + side],
            recv_sem=frecv.at[rs, 2 * d + side], device_id={axis: moved(axis, 2 * side - 1)},
            device_id_type=MESH)

    def field(ref, t):
        return [[ref[ri, s, :, t] for s in range(4)] for ri in range(2)]

    def keep(ref, t, total):
        for ri in range(2):
            for s in range(4):
                ref[ri, s, :, t] = total[ri][s]

    def build_null():
        loads[3].wait()
        for t in range(2):
            for x in range(4):
                nv[:, t, 2 * x:2 * x + 2, :] = null[:, x, t]

    def build_null_transposed():
        for ri in range(2):
            half = nv[12 * ri:12 * ri + 12].reshape(192, 192)
            nvt[192 * ri:192 * ri + 192, :] = half.T

    def build_coarse():
        for d in range(3):
            low_copy(d).wait()
        ff[...] = jnp.zeros_like(ff)
        fb[...] = jnp.zeros_like(fb)
        zero = jnp.zeros((24, 104), F32)

        def piece(ref, base, y):
            return jnp.concatenate([ref[pl.ds(base + y, 24, stride=2), :] * basis_scale, zero], axis=1)

        def placed(value, at):
            return value if at == 0 else pltpu.roll(value, at, 1)

        for y in range(2):
            blocks = []
            for direction in (0, 1, 3, 4, 2):
                blocks.append([piece(coarse, direction * 96 + ri * 48, y) for ri in range(2)])
            for ro in range(2):
                for tile in range(3):
                    total = None
                    for j in range(2):
                        if 2 * tile + j > 4:
                            continue
                        mr, mi = blocks[2 * tile + j]
                        first, second = (mr, -mi) if ro == 0 else (mi, mr)
                        part = placed(first, 64 * j) + placed(second, 64 * j + 32)
                        total = part if total is None else total + part
                    ff[64 * y + 32 * ro:64 * y + 32 * ro + 24, 128 * tile:128 * tile + 128] = total
        for block in range(4):
            parts = []
            for y in range(2):
                if block == 0:
                    parts.append([piece(coarse, 2 * 96 + ri * 48, 1 - y) for ri in range(2)])
                else:
                    parts.append([piece(low.at[block - 1], ri * 48, y) for ri in range(2)])
            for ri in range(2):
                total = None
                for y in range(2):
                    mr, mi = parts[y]
                    first, second = (mr, -mi) if ri == 0 else (mi, mr)
                    part = placed(first, 64 * y) + placed(second, 64 * y + 32)
                    total = part if total is None else total + part
                fb[64 * block + 32 * ri:64 * block + 32 * ri + 24, :] = total

    even = (iota((3, 8, 128), 1) & 1) == 0

    def start(f, ls, rs):
        v = field(f, 0)
        down = project(v, 3, -1.0)
        own_up = link_mul(links, 3, 0, project(v, 3, 1.0), True)
        v = field(f, 1)
        own_down = project(v, 3, -1.0)
        up = link_mul(links, 3, 1, project(v, 3, 1.0), True)
        for ri in range(2):
            for a in range(2):
                sendt[ls, 0, ri, a] = down[ri][a]
                sendt[ls, 1, ri, a] = up[ri][a]
                ht[ls, ri, a] = own_down[ri][a]
                qt[ls, ri, a] = own_up[ri][a]
        face_copy(2, 0, ls, rs).start()
        face_copy(2, 1, ls, rs).start()
        for t in range(2):
            v = field(f, t)
            down = project(v, 0, -1.0)
            up = link_mul(links, 0, t, project(v, 0, 1.0), True)
            for ri in range(2):
                for a in range(2):
                    j = 2 * (2 * a + t)
                    sendx[ls, 0, 3 * ri:3 * ri + 3, j:j + 2, :] = down[ri][a][:, 0:2]
                    sendx[ls, 1, 3 * ri:3 * ri + 3, j:j + 2, :] = up[ri][a][:, 6:8]
                    hx[ls, ri, a, :, t] = pltpu.roll(down[ri][a], 6, 1)
                    qx[ls, ri, a, :, t] = pltpu.roll(up[ri][a], 2, 1)
        face_copy(0, 0, ls, rs).start()
        face_copy(0, 1, ls, rs).start()
        downs, ups = [], []
        for t in range(2):
            v = field(f, t)
            downs.append(project(v, 2, -1.0))
            ups.append(link_mul(links, 2, t, project(v, 2, 1.0), True))
        for ri in range(2):
            for a in range(2):
                for t in range(2):
                    hz[ls, ri, a, :, t] = pltpu.roll(downs[t][ri][a], 7, 1)
                    qz[ls, ri, a, :, t] = pltpu.roll(ups[t][ri][a], 1, 1)
                sendz[ls, 0, ri, a] = jnp.where(even, downs[0][ri][a], pltpu.roll(downs[1][ri][a], 1, 1))
                sendz[ls, 1, ri, a] = jnp.where(even, pltpu.roll(ups[0][ri][a], 7, 1), ups[1][ri][a])
        face_copy(1, 0, ls, rs).start()
        face_copy(1, 1, ls, rs).start()

        lane = iota((3, 8, 128), 2)
        ypos = lane & 7
        below = jnp.where(lane < 8, fifth_hop * wall_mass, -fifth_hop).astype(F32)
        above = jnp.where(lane >= 120, fifth_hop * wall_mass, -fifth_hop).astype(F32)
        for t in range(2):
            v = field(f, t)
            total = [[None] * 4, [None] * 4]
            for ri in range(2):
                for s in range(4):
                    if s < 2:
                        side = below * pltpu.roll(v[ri][s], 8, 2)
                    else:
                        side = above * pltpu.roll(v[ri][s], 120, 2)
                    total[ri][s] = site_mass * v[ri][s] + side
            h = each(lambda w: jnp.where(ypos == 7, pltpu.roll(w, 7, 2), pltpu.roll(w, 127, 2)), project(v, 1, -1.0))
            rebuild(total, link_mul(links, 1, t, h, False), 1, -1.0)
            h = link_mul(links, 1, t, project(v, 1, 1.0), True)
            h = each(lambda w: jnp.where(ypos == 0, pltpu.roll(w, 121, 2), pltpu.roll(w, 1, 2)), h)
            rebuild(total, h, 1, 1.0)
            if t == 0:
                h = [[ht[ls, ri, a] for a in range(2)] for ri in range(2)]
                rebuild(total, link_mul(links, 3, 0, h, False), 3, -1.0)
            else:
                rebuild(total, [[qt[ls, ri, a] for a in range(2)] for ri in range(2)], 3, 1.0)
            keep(acc.at[ls], t, total)

    def finish(ls, rs, emit):
        face_copy(1, 0, ls, rs).wait()
        face_copy(1, 1, ls, rs).wait()
        for t in range(2):
            total = field(acc.at[ls], t)
            h = [[None, None], [None, None]]
            q = [[None, None], [None, None]]
            for ri in range(2):
                for a in range(2):
                    came, back = recvz[rs, 0, ri, a], recvz[rs, 1, ri, a]
                    if t == 0:
                        came = pltpu.roll(came, 1, 1)
                    else:
                        back = pltpu.roll(back, 7, 1)
                    h[ri][a] = jnp.where(even, hz[ls, ri, a, :, t], came)
                    q[ri][a] = jnp.where(even, back, qz[ls, ri, a, :, t])
            rebuild(total, link_mul(links, 2, t, h, False), 2, -1.0)
            rebuild(total, q, 2, 1.0)
            keep(acc.at[ls], t, total)
        face_copy(0, 0, ls, rs).wait()
        face_copy(0, 1, ls, rs).wait()
        for ri in range(2):
            for a in range(2):
                for t in range(2):
                    j = 2 * (2 * a + t)
                    hx[ls, ri, a, :, t, 6:8, :] = recvx[rs, 0, 3 * ri:3 * ri + 3, j:j + 2, :]
                    qx[ls, ri, a, :, t, 0:2, :] = recvx[rs, 1, 3 * ri:3 * ri + 3, j:j + 2, :]
        for t in range(2):
            total = field(acc.at[ls], t)
            h = [[hx[ls, ri, a, :, t] for a in range(2)] for ri in range(2)]
            rebuild(total, link_mul(links, 0, t, h, False), 0, -1.0)
            rebuild(total, [[qx[ls, ri, a, :, t] for a in range(2)] for ri in range(2)], 0, 1.0)
            keep(acc.at[ls], t, total)
        face_copy(2, 0, ls, rs).wait()
        face_copy(2, 1, ls, rs).wait()
        for t in range(2):
            total = field(acc.at[ls], t)
            if t == 0:
                rebuild(total, [[recvt[rs, 1, ri, a] for a in range(2)] for ri in range(2)], 3, 1.0)
            else:
                h = [[recvt[rs, 0, ri, a] for a in range(2)] for ri in range(2)]
                rebuild(total, link_mul(links, 3, 1, h, False), 3, -1.0)
            emit(t, total)

    def advance(k):
        alpha = jnp.float32(ALPHA[0])
        beta = jnp.float32(BETA[0])
        for at in range(1, 2 * DEG):
            alpha = jnp.where(k == at, jnp.float32(ALPHA[at]), alpha)
            beta = jnp.where(k == at, jnp.float32(BETA[at]), beta)

        def emit(t, total):
            for ri in range(2):
                for s in range(4):
                    left = r[ri, s, :, t] - total[ri][s]
                    step = alpha * p[ri, s, :, t] + beta * left
                    r[ri, s, :, t] = left
                    p[ri, s, :, t] = step
                    u[ri, s, :, t] = u[ri, s, :, t] + step

        return emit

    def round_of(k, hooks):
        slot = lax.rem(k, 2)
        start(p, 0, slot)
        for at, hook in hooks:
            pl.when(k == at)(hook)
        finish(0, slot, advance(k))

    def first_half(k, carry):
        round_of(k, ((0, build_null), (1, build_null_transposed), (2, build_coarse)))
        return carry

    def second_half(k, carry):
        round_of(k, ())
        return carry

    for d in range(3):
        low_copy(d).start()
    lax.fori_loop(0, DEG, first_half, 0)

    diagonal = (iota((192, 256), 0) & 7) == (iota((192, 256), 1) & 7)
    selector = jnp.where(
        ((lane8 >> 5) == (row8 & 3)) & (((lane8 & 7) >> 2) == (row8 >> 2)), 1.0, 0.0).astype(F32)
    fold = jnp.where((iota((32, 192), 1) >> 3) == iota((32, 192), 0), 1.0, 0.0).astype(F32)
    unfold = jnp.where((iota((192, 32), 0) >> 3) == iota((192, 32), 1), 1.0, 0.0).astype(F32)
    both = jnp.concatenate([r[0].reshape(192, 128), r[1].reshape(192, 128)], axis=1)
    prod = dot(nvt[...], both)
    real = prod[0:192, 0:128] + prod[192:384, 128:256]
    imag = prod[0:192, 128:256] - prod[192:384, 0:128]
    kept = jnp.where(diagonal, jnp.concatenate([real, imag], axis=1), 0.0)
    summed = dot(fold, kept)
    stacked = jnp.concatenate([summed[:, 0:128], summed[:, 128:256]] * 2, axis=0)
    basis[0] = dot(selector, stacked, ((1,), (1,)))

    def coarse_copy(step, d, side):
        axis = AXES[d][1]
        return pltpu.make_async_remote_copy(
            src_ref=basis.at[step], dst_ref=crecv.at[step, 2 * d + side], send_sem=csend.at[step, 2 * d + side],
            recv_sem=crsem.at[step, 2 * d + side], device_id={axis: moved(axis, 2 * side - 1)},
            device_id_type=MESH)

    low_half = lane8 < 64

    def prolong(step):
        spread = dot(basis[step], selector, ((0,), (0,)))
        paired = jnp.concatenate([spread[0:32], spread[32:64]], axis=1)
        weights = jnp.where(diagonal, dot(unfold, paired), 0.0)
        prod = dot(nv[...].reshape(384, 192), weights)
        fields[step, 0] = (prod[0:192, 0:128] - prod[192:384, 128:256]).reshape(4, 3, 2, 8, 128)
        fields[step, 1] = (prod[0:192, 128:256] + prod[192:384, 0:128]).reshape(4, 3, 2, 8, 128)

    def into(index):
        return lambda t, total: keep(fields.at[index], t, total)

    def finish_first(step):
        finish(lax.rem(step, 2), 2 + step, into(5 + step))

    def finish_second(step):
        finish(2 + lax.rem(step, 2), 6 + step, into(9 + step))

    def start_second(step):
        start(fields.at[4 + step], 2 + lax.rem(step, 2), 6 + step)

    def coarse_step(step, carry):
        for d in (2, 0, 1):
            for side in range(2):
                coarse_copy(step, d, side).start()
        prolong(step)
        start(fields.at[step], lax.rem(step, 2), 2 + step)

        @pl.when(step >= 1)
        def _():
            finish_first(step - 1)
            finish_second(step - 1)

        start_second(step)

        own = basis[step]
        other = pltpu.roll(own, 4, 0)
        layer = row8 & 3
        from_below = jnp.where(layer == 0, -wall_mass * pltpu.roll(own, 5, 0), pltpu.roll(own, 1, 0))
        from_above = jnp.where(layer == 3, -wall_mass * pltpu.roll(own, 3, 0), pltpu.roll(own, 7, 0))
        local = (-coarse_fifth * basis_scale) * (from_below + from_above)
        for d in range(3):
            for side in range(2):
                coarse_copy(step, d, side).wait()
        got = [crecv[step, j] for j in range(6)]
        ahead = jnp.concatenate(
            [jnp.where(low_half, own, got[0]), jnp.where(low_half, got[2], got[4]), other], axis=1)
        behind = jnp.concatenate(
            [jnp.where(low_half, other, got[1]), jnp.where(low_half, got[3], got[5])], axis=1)
        out = dot(ahead, ff[...], ((1,), (1,))) + dot(behind, fb[...])
        out = jnp.where((row8 < 4) == low_half, out, pltpu.roll(out, 64, 1))
        basis[step + 1] = out + local
        return carry

    lax.fori_loop(0, CITERS, coarse_step, 0)

    size = CITERS + 1
    vectors = [basis[i] for i in range(size)]
    sign = jnp.where((lane8 & 32) == 0, 1.0, -1.0).astype(F32)
    turned = [sign * pltpu.roll(v, 32, 1) for v in vectors]
    entries = [(i, j, 0) for i in range(size) for j in range(i, size)]
    entries += [(i, j, 1) for i in range(size) for j in range(i + 1, size)]
    none = jnp.zeros((8, 128), F32)
    products = [vectors[i] * (vectors[j] if part == 0 else turned[j]) for i, j, part in entries]
    products = jnp.stack(products + [none] * (32 - len(products)))
    rows = jnp.sum(jnp.where(low_half[None], products, 0.0), axis=1)
    padded = jnp.concatenate([rows, jnp.zeros((96, 128), F32)], axis=0)
    sums = dot(jnp.ones((8, 128), F32), padded, ((1,), (1,)))

    def sum_copies(phase):
        return [pltpu.make_async_remote_copy(
            src_ref=ar_send.at[phase], dst_ref=ar_recv.at[phase, by], send_sem=asend.at[phase, by],
            recv_sem=arsem.at[phase, by], device_id=partner, device_id_type=MESH)
            for by, partner in enumerate(groups[phase])]

    def send_sums(phase, value):
        ar_send[phase] = value
        for copy in sum_copies(phase):
            copy.start()

    def take_sums(phase):
        parts = [ar_send[phase]]
        for by, copy in enumerate(sum_copies(phase)):
            copy.wait()
            parts.append(ar_recv[phase, by])
        while len(parts) > 1:
            parts = [parts[i] + parts[i + 1] if i + 1 < len(parts) else parts[i] for i in range(0, len(parts), 2)]
        return parts[0]

    send_sums(0, sums)
    finish_first(CITERS - 1)
    start_second(CITERS)
    finish_second(CITERS - 1)
    send_sums(1, take_sums(0))
    finish_second(CITERS)
    sums = take_sums(1)

    moments = [[None] * size for _ in range(size)]
    for number, (i, j, part) in enumerate(entries):
        value = jnp.broadcast_to(sums[:, number:number + 1], (8, 128))
        moments[i][j] = (value, none) if part == 0 else (moments[i][j][0], value)
    one = jnp.ones((8, 128), F32)
    coef = [(one, none)]
    answer = [(none, none)] * CITERS
    grow = 1.0 / basis_scale
    for step in range(CITERS):
        m00, m11 = moments[0][0][0], moments[1][1][0]
        m01r, m01i = moments[0][1]
        bottom = 1.0 / ((coarse_mass * coarse_mass) * m00 + (2.0 * coarse_mass * grow) * m01r + (grow * grow) * m11)
        ar = (coarse_mass * m00 + grow * m01r) * bottom
        ai = (-grow * m01i) * bottom
        for i, (cr, ci) in enumerate(coef):
            answer[i] = (answer[i][0] + (ar * cr - ai * ci), answer[i][1] + (ar * ci + ai * cr))
        kr, ki = 1.0 - coarse_mass * ar, -coarse_mass * ai
        dr, di = -grow * ar, -grow * ai
        kk, dd = kr * kr + ki * ki, dr * dr + di * di
        wr, wi = kr * dr + ki * di, kr * di - ki * dr
        fresh = [[None] * size for _ in range(size)]
        for m in range(size - 1 - step):
            for n in range(m, size - 1 - step):
                hr, hi = moments[m][n]
                nr, ni = moments[m][n + 1]
                fr, fi = moments[m + 1][n + 1]
                if m == n:
                    fresh[m][n] = ((kk * hr + dd * fr) + 2.0 * (wr * nr - wi * ni), none)
                else:
                    lr, li = moments[m + 1][n]
                    fresh[m][n] = ((kk * hr + dd * fr) + (wr * nr - wi * ni) + (wr * lr + wi * li),
                                   (kk * hi + dd * fi) + (wr * ni + wi * nr) + (wr * li - wi * lr))
        moments = fresh
        grown = [(kr * cr - ki * ci, kr * ci + ki * cr) for cr, ci in coef] + [(none, none)]
        for i, (cr, ci) in enumerate(coef):
            gr, gi = grown[i + 1]
            grown[i + 1] = (gr + (dr * cr - di * ci), gi + (dr * ci + di * cr))
        coef = grown

    alpha, beta = PAIRS[0]
    for t in range(2):
        for s in range(4):
            parts = [[fields[4, ri, s, :, t], fields[9, ri, s, :, t], u[ri, s, :, t]] for ri in range(2)]
            for i in range(CITERS):
                cr, ci = answer[i][0][None], answer[i][1][None]
                for part, at in ((0, 5 + i), (1, 10 + i), (2, i)):
                    fr, fi = fields[at, 0, s, :, t], fields[at, 1, s, :, t]
                    re, im = cr * fr - ci * fi, cr * fi + ci * fr
                    parts[0][part] = plus(parts[0][part], re, 1.0 if part == 2 else -1.0)
                    parts[1][part] = plus(parts[1][part], im, 1.0 if part == 2 else -1.0)
            for ri in range(2):
                left, through, result = parts[ri]
                step = START * left
                left = left - START * through
                after = alpha * step + beta * left
                r[ri, s, :, t] = left
                p[ri, s, :, t] = after
                u[ri, s, :, t] = result + step + after

    found = none
    for i in range(CITERS):
        found = found + (answer[i][0] * vectors[i] - answer[i][1] * turned[i])
    for ri in range(2):
        part = found if ri == 0 else pltpu.roll(found, 96, 1)
        for c in range(4):
            for y in range(2):
                at = 8 * ri + 2 * c + y
                e_out[at:at + 1, :] = part[4 * y + c:4 * y + c + 1, 0:24]

    lax.fori_loop(DEG + 2, 2 * DEG, second_half, 0)
    for t in range(2):
        for x in range(4):
            u_out[:, 4 * x + 2 * t:4 * x + 2 * t + 2, :] = u[:, :, :, t, 2 * x:2 * x + 2, :].reshape(24, 2, 128)


def body(sizes, source_field, gauge_links, null_vectors, coarse_links):
    hbm = pl.BlockSpec(memory_space=pl.ANY)
    vmem = pl.BlockSpec(memory_space=pltpu.VMEM)
    half = (4, 2, 2, 3, 2, 8, 128)
    full = (2, 4, 3, 2, 8, 128)
    most = max(sizes["ta"], sizes["grp"] * sizes["gz"]) - 1
    arguments = [(24, 16, 128), (72, 16, 8), (24, 4, 2, 2, 192), (480, 24)]
    shapes = arguments + [full, full, (14,) + full, (4,) + full, (4, 2, 3, 3, 2, 8, 128), (72, 2, 8, 8),
                          half, half, half, half, (4, 2, 2, 3, 8, 128), (4, 2, 2, 3, 8, 128),
                          (4, 2, 6, 8, 128), (4, 2, 2, 2, 3, 8, 128), (4, 2, 2, 2, 3, 8, 128),
                          (11, 2, 6, 8, 128), (11, 2, 2, 2, 3, 8, 128), (11, 2, 2, 2, 3, 8, 128),
                          (24, 2, 8, 192), (384, 192), (3, 96, 24), (128, 384), (256, 128), (CITERS + 1, 8, 128),
                          (CITERS, 6, 8, 128), (2, 8, 128), (2, most, 8, 128)]
    sems = [(4,), (4, 6), (11, 6), (3,), (3,), (CITERS, 6), (CITERS, 6), (2, most), (2, most)]
    out, found = pl.pallas_call(
        functools.partial(kernel, sizes),
        out_shape=(jax.ShapeDtypeStruct((24, 16, 128), F32), jax.ShapeDtypeStruct((16, 24), F32)),
        in_specs=[hbm] * 4,
        out_specs=(vmem, vmem),
        scratch_shapes=[pltpu.VMEM(shape, F32) for shape in shapes]
        + [pltpu.SemaphoreType.DMA(shape) for shape in sems],
        compiler_params=pltpu.CompilerParams(
            collective_id=0, has_side_effects=True, vmem_limit_bytes=56 * 1024 * 1024),
    )(
        source_field.reshape(arguments[0]),
        gauge_links.reshape(arguments[1]),
        null_vectors.reshape(arguments[2]),
        coarse_links.transpose(0, 1, 2, 4, 5, 6, 7, 3).reshape(arguments[3]),
    )
    found = found.reshape(2, 4, 2, 24).transpose(0, 3, 1, 2)
    return out.reshape(source_field.shape), found.reshape(2, 24, 4, 1, 1, 1, 2)


def solution(mesh):
    sizes = {axis: mesh.shape[axis] for axis in ("grp", "ta", "gz")}
    placed = (
        P(None, None, None, "grp", "ta", "gz", None),
        P(None, None, None, None, "grp", "ta", "gz", None),
        P(None, None, None, "grp", "ta", "gz", None),
        P(None, None, None, None, "grp", "ta", "gz", None),
    )
    return jax.shard_map(
        functools.partial(body, sizes),
        mesh=mesh,
        in_specs=placed,
        out_specs=(
            P(None, None, None, "grp", "ta", "gz", None),
            P(None, None, None, "grp", "ta", "gz", None),
        ),
        check_vma=False,
    )
```

time: 95.8 us -> 77.7 us (0.81)
  Pallas kernels: 89.6 us -> 74.7 us
  local copies, waits for them, and re-layouts: 5.28 us -> 2.22 us
    pallas_call x1, Pallas kernels: 89.6 us -> 74.7 us  [body(): pl.pallas_call(functools.partial(kernel, sizes), out_shape=(jax.ShapeDtyp...]
    unnamed x10 -> x4, local copies, waits for them, and re-layouts: 5.2 us -> 2.22 us
where the time goes in v1:
time: 77.7 us; the launch traced here: 77.6 us
  Pallas kernels  74.7 us (96%)
  local copies, waits for them, and re-layouts  2.22 us (3%)
    pallas_call x1, Pallas kernels, body(): pl.pallas_call(functools.partial(kernel, sizes), out_shape=(jax.ShapeDtyp...  74.7 us
    unnamed x4, local copies, waits for them, and re-layouts  2.22 us

profile of v1, /device:TPU:1, one launch (start us, length us, event | category | flops | bytes accessed | tf_op | source)
XLA Modules:
  0.0 77.6 jit_solution(6217208124133538181)
XLA Ops:
  0.6 74.7 %shard_map.59 = (f32[24,16,128]{2,1,0:T(8,128)}, f32[16,24]{1,0:T(8,128)}) custom-call(f32[24,16,128]{2,1,0:T(8,128)} %bitcast.16, f32[72,16,8]{2,1,0:T(8,128)} %bitcast.12, f32[24,4,2,2,192]{4,3,2,1,0:T(2,128)} %bitcast.13, f32[480,24]{1,0:T(8,128)} %bitcast.14), custom_call_target="tpu_custom_call" | custom-call | tf_op jit(solution)/shard_map/pallas_call | solution.py:598
  75.4 0.0 copy-start
  75.4 1.6 %copy.8 = f32[2,4,3,4,2,2,128]{6,5,4,3,2,1,0:T(2,128)} copy(f32[2,4,3,4,2,2,128]{6,5,4,3,2,1,0:T(2,128)} %bitcast.15) | data formatting | bytes 393216
  77.0 0.0 copy-done
  77.0 0.6 copy.9
Async XLA Ops:
  75.4 1.6 %copy-start = (f32[16,24]{1,0:T(8,128)S(1)}, f32[16,24]{1,0:T(8,128)}, u32[]{:S(2)}) copy-start(f32[16,24]{1,0:T(8,128)} %get-tuple-element.5) | copy-start | bytes 4612

commit v2 on v1

--- a/solution.py
+++ b/solution.py
@@ -107,13 +107,52 @@
     )
 
 
+def halves(a):
+    high = a.astype(jnp.bfloat16)
+    return high, (a - high.astype(F32)).astype(jnp.bfloat16)
+
+
+def dot_halves(a, b):
+    return sum(jnp.dot(a[i], b[j], preferred_element_type=F32) for i, j in ((1, 0), (0, 1), (0, 0)))
+
+
+def pick(ones, b):
+    ones = ones.astype(jnp.bfloat16)
+    high, low = halves(b)
+    return jnp.dot(ones, low, preferred_element_type=F32) + jnp.dot(ones, high, preferred_element_type=F32)
+
+
 def iota(shape, dim):
     return lax.broadcasted_iota(jnp.int32, shape, dim)
 
 
+def wrap(sizes, disp):
+    return tuple(by % sizes[axis] for by, (_, axis) in zip(disp, AXES))
+
+
+STENCIL = (((0, 0, 0), 0), ((0, 0, 0), 1), ((1, 0, 0), 0), ((-1, 0, 0), 0),
+           ((0, 1, 0), 0), ((0, -1, 0), 0), ((0, 0, 1), 0), ((0, 0, -1), 0))
+CHUNKS = ((0, 4), (4, 8))
+
+
+def reach(sizes):
+    keys = []
+    for first, flip in STENCIL:
+        for second, again in STENCIL:
+            key = (wrap(sizes, [i + j for i, j in zip(first, second)]), flip ^ again)
+            if key not in keys:
+                keys.append(key)
+    far = []
+    for disp, _ in keys:
+        if any(disp) and disp not in far:
+            far.append(disp)
+    return keys, far
+
+
 def kernel(sizes, src_in, gauge_in, null_in, coarse_in, u_out, e_out, src, gauge, null, coarse, p, u, fields, acc, links, g8,
-           hx, qx, hz, qz, ht, qt, sendx, sendz, sendt, recvx, recvz, recvt, nv, nvt, low, ff, fb, basis, crecv, ar_send,
-           ar_recv, isem, fsend, frecv, lsend, lrecv, csend, crsem, asend, arsem):
+           hx, qx, hz, qz, ht, qt, sendx, sendz, sendt, recvx, recvz, recvt, nv, nvs, nvt, low, ff, fb, wide, rows24, wrecv,
+           twice, basis, crecv, ar_send, ar_recv, isem, fsend, frecv, lsend, lrecv, wsend, wrsem, csend, crsem, asend, arsem):
+    keys, far = reach(sizes)
     me = {axis: lax.axis_index(axis) for axis in ("grp", "ta", "gz")}
     plane = sizes["grp"] * sizes["gz"]
     spot = me["grp"] * sizes["gz"] + me["gz"]
@@ -127,8 +166,15 @@
 
     groups = ([{"ta": moved("ta", by)} for by in range(1, sizes["ta"])], [in_plane(by) for by in range(1, plane)])
 
+    def at(disp):
+        return {axis: moved(axis, by) for by, (_, axis) in zip(disp, AXES)}
+
+    def back(disp):
+        return at(wrap(sizes, [-by for by in disp]))
+
     barrier = pltpu.get_barrier_semaphore()
-    for partner in groups[0] + groups[1]:
+    partners = [at(disp) for disp, _ in STENCIL if any(disp)]
+    for partner in partners:
         pl.semaphore_signal(barrier, inc=1, device_id=partner, device_id_type=MESH)
 
     loads = [pltpu.make_async_copy(a, b, isem.at[i]) for i, (a, b) in enumerate(
@@ -154,7 +200,7 @@
             u[:, :, :, t, 2 * x:2 * x + 2, :] = rows * START
     loads[2].wait()
 
-    pl.semaphore_wait(barrier, len(groups[0]) + len(groups[1]))
+    pl.semaphore_wait(barrier, len(partners))
 
     def low_copy(d):
         return pltpu.make_async_remote_copy(
@@ -189,7 +235,10 @@
     def build_null_transposed():
         for ri in range(2):
             half = nv[12 * ri:12 * ri + 12].reshape(192, 192)
-            nvt[192 * ri:192 * ri + 192, :] = half.T
+            for part, value in enumerate(halves(half)):
+                nvs[part, 192 * ri:192 * ri + 192, :] = value
+            for part, value in enumerate(halves(half.T)):
+                nvt[part, 192 * ri:192 * ri + 192, :] = value
 
     def build_coarse():
         for d in range(3):
@@ -234,6 +283,49 @@
                     part = placed(first, 64 * y) + placed(second, 64 * y + 32)
                     total = part if total is None else total + part
                 fb[64 * block + 32 * ri:64 * block + 32 * ri + 24, :] = total
+        flat = ff[...].T
+        order = (flat[0:64], flat[256:320] + fb[0:64], flat[64:128], fb[64:128], flat[128:192], fb[128:192],
+                 flat[192:256], fb[192:256])
+        for block, rows in enumerate(order):
+            wide[64 * block:64 * block + 64, :] = rows
+            rows24[block] = rows[0:24]
+
+    def row_copy(block, chunk):
+        first, last = CHUNKS[chunk]
+        return pltpu.make_async_remote_copy(
+            src_ref=rows24.at[first:last], dst_ref=wrecv.at[block - 2, first:last], send_sem=wsend.at[block - 2, chunk],
+            recv_sem=wrsem.at[block - 2, chunk], device_id=back(STENCIL[block][0]), device_id_type=MESH)
+
+    def send_rows(chunk):
+        def send():
+            for block in range(2, 8):
+                row_copy(block, chunk).start()
+
+        return send
+
+    def build_null_and_send():
+        send_rows(0)()
+        build_null_transposed()
+
+    def build_twice():
+        twice[...] = jnp.zeros_like(twice)
+        for block, (disp, flip) in enumerate(STENCIL):
+            if block >= 2:
+                for chunk in range(len(CHUNKS)):
+                    row_copy(block, chunk).wait()
+            mine = wide[64 * block:64 * block + 64, :]
+            left = iota((64, 128), 1) < 64
+            upper, lower = jnp.where(left, mine, 0.0), jnp.where(left, 0.0, mine)
+            weights = jnp.concatenate([lower, upper] if flip else [upper, lower], axis=0)
+            theirs = rows24[...] if block < 2 else wrecv[block - 2]
+            product = dot(theirs.reshape(8 * 24, 128), weights)
+            real_lane = (iota((8 * 24, 128), 1) & 32) == 0
+            turned = jnp.where(real_lane, -pltpu.roll(product, 96, 1), pltpu.roll(product, 32, 1))
+            for other, (further, again) in enumerate(STENCIL):
+                key = (wrap(sizes, [i + j for i, j in zip(disp, further)]), flip ^ again)
+                base = 64 * keys.index(key)
+                for ri, part in ((0, product), (1, turned)):
+                    twice[base + 32 * ri:base + 32 * ri + 24, :] += part[24 * other:24 * other + 24]
 
     even = (iota((3, 8, 128), 1) & 1) == 0
 
@@ -376,7 +468,7 @@
         finish(0, slot, advance(k))
 
     def first_half(k, carry):
-        round_of(k, ((0, build_null), (1, build_null_transposed), (2, build_coarse)))
+        round_of(k, ((0, build_null), (1, build_coarse), (2, build_null_and_send), (3, send_rows(1))))
         return carry
 
     def second_half(k, carry):
@@ -393,77 +485,94 @@
     fold = jnp.where((iota((32, 192), 1) >> 3) == iota((32, 192), 0), 1.0, 0.0).astype(F32)
     unfold = jnp.where((iota((192, 32), 0) >> 3) == iota((192, 32), 1), 1.0, 0.0).astype(F32)
     both = jnp.concatenate([r[0].reshape(192, 128), r[1].reshape(192, 128)], axis=1)
-    prod = dot(nvt[...], both)
+    prod = dot_halves((nvt[0], nvt[1]), halves(both))
     real = prod[0:192, 0:128] + prod[192:384, 128:256]
     imag = prod[0:192, 128:256] - prod[192:384, 0:128]
     kept = jnp.where(diagonal, jnp.concatenate([real, imag], axis=1), 0.0)
-    summed = dot(fold, kept)
+    summed = pick(fold, kept)
     stacked = jnp.concatenate([summed[:, 0:128], summed[:, 128:256]] * 2, axis=0)
     basis[0] = dot(selector, stacked, ((1,), (1,)))
 
-    def coarse_copy(step, d, side):
-        axis = AXES[d][1]
-        return pltpu.make_async_remote_copy(
-            src_ref=basis.at[step], dst_ref=crecv.at[step, 2 * d + side], send_sem=csend.at[step, 2 * d + side],
-            recv_sem=crsem.at[step, 2 * d + side], device_id={axis: moved(axis, 2 * side - 1)},
-            device_id_type=MESH)
+    def coarse_copies(step):
+        return [pltpu.make_async_remote_copy(
+            src_ref=basis.at[2 * step], dst_ref=crecv.at[step, i], send_sem=csend.at[step, i],
+            recv_sem=crsem.at[step, i], device_id=back(disp), device_id_type=MESH)
+            for i, disp in enumerate(far)]
 
     low_half = lane8 < 64
 
     def prolong(step):
         spread = dot(basis[step], selector, ((0,), (0,)))
         paired = jnp.concatenate([spread[0:32], spread[32:64]], axis=1)
-        weights = jnp.where(diagonal, dot(unfold, paired), 0.0)
-        prod = dot(nv[...].reshape(384, 192), weights)
+        weights = jnp.where(diagonal, pick(unfold, paired), 0.0)
+        prod = dot_halves((nvs[0], nvs[1]), halves(weights))
         fields[step, 0] = (prod[0:192, 0:128] - prod[192:384, 128:256]).reshape(4, 3, 2, 8, 128)
         fields[step, 1] = (prod[0:192, 128:256] + prod[192:384, 0:128]).reshape(4, 3, 2, 8, 128)
 
-    def into(index):
-        return lambda t, total: keep(fields.at[index], t, total)
-
-    def finish_first(step):
-        finish(lax.rem(step, 2), 2 + step, into(5 + step))
-
-    def finish_second(step):
-        finish(2 + lax.rem(step, 2), 6 + step, into(9 + step))
-
-    def start_second(step):
-        start(fields.at[4 + step], 2 + lax.rem(step, 2), 6 + step)
-
-    def coarse_step(step, carry):
-        for d in (2, 0, 1):
-            for side in range(2):
-                coarse_copy(step, d, side).start()
-        prolong(step)
-        start(fields.at[step], lax.rem(step, 2), 2 + step)
-
-        @pl.when(step >= 1)
-        def _():
-            finish_first(step - 1)
-            finish_second(step - 1)
-
-        start_second(step)
-
-        own = basis[step]
-        other = pltpu.roll(own, 4, 0)
+    def begin(f):
+        start(fields.at[f], 1 + f, 2 + f)
+
+    def end(f):
+        finish(1 + f, 2 + f, lambda t, total: keep(fields.at[5 + f], t, total))
+
+    def across(own):
         layer = row8 & 3
         from_below = jnp.where(layer == 0, -wall_mass * pltpu.roll(own, 5, 0), pltpu.roll(own, 1, 0))
         from_above = jnp.where(layer == 3, -wall_mass * pltpu.roll(own, 3, 0), pltpu.roll(own, 7, 0))
-        local = (-coarse_fifth * basis_scale) * (from_below + from_above)
-        for d in range(3):
-            for side in range(2):
-                coarse_copy(step, d, side).wait()
-        got = [crecv[step, j] for j in range(6)]
-        ahead = jnp.concatenate(
-            [jnp.where(low_half, own, got[0]), jnp.where(low_half, got[2], got[4]), other], axis=1)
-        behind = jnp.concatenate(
-            [jnp.where(low_half, other, got[1]), jnp.where(low_half, got[3], got[5])], axis=1)
-        out = dot(ahead, ff[...], ((1,), (1,))) + dot(behind, fb[...])
-        out = jnp.where((row8 < 4) == low_half, out, pltpu.roll(out, 64, 1))
-        basis[step + 1] = out + local
+        return (-coarse_fifth * basis_scale) * (from_below + from_above)
+
+    def gathered(step, wanted):
+        own = basis[2 * step]
+        parts = []
+        for disp, flip in wanted:
+            disp = wrap(sizes, disp)
+            part = crecv[step, far.index(disp)] if any(disp) else own
+            parts.append(pltpu.roll(part, 4, 0) if flip else part)
+        if len(parts) % 2:
+            parts.append(own)
+        return jnp.concatenate(
+            [jnp.where(low_half, parts[i], parts[i + 1]) for i in range(0, len(parts), 2)], axis=1)
+
+    def own_y(out):
+        return jnp.where((row8 < 4) == low_half, out, pltpu.roll(out, 64, 1))
+
+    def send_basis(step):
+        for copy in coarse_copies(step):
+            copy.start()
+
+    def take_basis(step):
+        for copy in coarse_copies(step):
+            copy.wait()
+        once = own_y(dot(gathered(step, STENCIL), wide[...]))
+        shifted = across(basis[2 * step])
+        basis[2 * step + 1] = once + shifted
+        return 2.0 * once + shifted
+
+    def take_second(step, first):
+        again = own_y(dot(gathered(step, keys), twice[...]))
+        basis[2 * step + 2] = again + across(first)
+
+    send_basis(0)
+    prolong(0)
+    begin(0)
+    begin(4)
+    build_twice()
+    take_second(0, take_basis(0))
+    send_basis(1)
+
+    def lift(f, carry):
+        prolong(f)
+        begin(f)
         return carry
 
-    lax.fori_loop(0, CITERS, coarse_step, 0)
+    lax.fori_loop(1, 3, lift, 0)
+    end(0)
+    begin(5)
+    end(4)
+    first = take_basis(1)
+    prolong(3)
+    begin(3)
+    take_second(1, first)
 
     size = CITERS + 1
     vectors = [basis[i] for i in range(size)]
@@ -499,11 +608,23 @@
         return parts[0]
 
     send_sums(0, sums)
-    finish_first(CITERS - 1)
-    start_second(CITERS)
-    finish_second(CITERS - 1)
+
+    def turn(f, carry):
+        end(f)
+        begin(5 + f)
+        return carry
+
+    def settle(f, carry):
+        end(f)
+        return carry
+
+    lax.fori_loop(1, 3, turn, 0)
+    end(5)
     send_sums(1, take_sums(0))
-    finish_second(CITERS)
+    end(3)
+    begin(8)
+    lax.fori_loop(6, 8, settle, 0)
+    end(8)
     sums = take_sums(1)
 
     moments = [[None] * size for _ in range(size)]
@@ -584,23 +705,25 @@
 def body(sizes, source_field, gauge_links, null_vectors, coarse_links):
     hbm = pl.BlockSpec(memory_space=pl.ANY)
     vmem = pl.BlockSpec(memory_space=pltpu.VMEM)
-    half = (4, 2, 2, 3, 2, 8, 128)
+    keys, far = reach(sizes)
+    most_rows = 64 * (len(keys) + len(keys) % 2)
+    half = (10, 2, 2, 3, 2, 8, 128)
     full = (2, 4, 3, 2, 8, 128)
     most = max(sizes["ta"], sizes["grp"] * sizes["gz"]) - 1
     arguments = [(24, 16, 128), (72, 16, 8), (24, 4, 2, 2, 192), (480, 24)]
-    shapes = arguments + [full, full, (14,) + full, (4,) + full, (4, 2, 3, 3, 2, 8, 128), (72, 2, 8, 8),
-                          half, half, half, half, (4, 2, 2, 3, 8, 128), (4, 2, 2, 3, 8, 128),
-                          (4, 2, 6, 8, 128), (4, 2, 2, 2, 3, 8, 128), (4, 2, 2, 2, 3, 8, 128),
+    shapes = arguments + [full, full, (14,) + full, (10,) + full, (4, 2, 3, 3, 2, 8, 128), (72, 2, 8, 8),
+                          half, half, half, half, (10, 2, 2, 3, 8, 128), (10, 2, 2, 3, 8, 128),
+                          (10, 2, 6, 8, 128), (10, 2, 2, 2, 3, 8, 128), (10, 2, 2, 2, 3, 8, 128),
                           (11, 2, 6, 8, 128), (11, 2, 2, 2, 3, 8, 128), (11, 2, 2, 2, 3, 8, 128),
-                          (24, 2, 8, 192), (384, 192), (3, 96, 24), (128, 384), (256, 128), (CITERS + 1, 8, 128),
-                          (CITERS, 6, 8, 128), (2, 8, 128), (2, most, 8, 128)]
-    sems = [(4,), (4, 6), (11, 6), (3,), (3,), (CITERS, 6), (CITERS, 6), (2, most), (2, most)]
+                          (24, 2, 8, 192), (2, 384, 192), (2, 384, 192), (3, 96, 24), (128, 384), (256, 128), (512, 128), (8, 24, 128), (6, 8, 24, 128),
+                          (most_rows, 128), (CITERS + 1, 8, 128), (2, len(far), 8, 128), (2, 8, 128), (2, most, 8, 128)]
+    sems = [(4,), (10, 6), (11, 6), (3,), (3,), (6, 2), (6, 2), (2, len(far)), (2, len(far)), (2, most), (2, most)]
     out, found = pl.pallas_call(
         functools.partial(kernel, sizes),
         out_shape=(jax.ShapeDtypeStruct((24, 16, 128), F32), jax.ShapeDtypeStruct((16, 24), F32)),
         in_specs=[hbm] * 4,
         out_specs=(vmem, vmem),
-        scratch_shapes=[pltpu.VMEM(shape, F32) for shape in shapes]
+        scratch_shapes=[pltpu.VMEM(shape, jnp.bfloat16 if shape == (2, 384, 192) else F32) for shape in shapes]
         + [pltpu.SemaphoreType.DMA(shape) for shape in sems],
         compiler_params=pltpu.CompilerParams(
             collective_id=0, has_side_effects=True, vmem_limit_bytes=56 * 1024 * 1024),

time: 77.7 us -> 76.8 us (0.988)
  Pallas kernels: 74.7 us -> 73.8 us
    pallas_call x1, Pallas kernels: 74.7 us -> 73.8 us  [body(): pl.pallas_call(functools.partial(kernel, sizes), out_shape=(jax.ShapeDtyp...]
where the time goes in v2:
time: 76.8 us; the launch traced here: 76.6 us
  Pallas kernels  73.8 us (96%)
  local copies, waits for them, and re-layouts  2.22 us (3%)
    pallas_call x1, Pallas kernels, body(): pl.pallas_call(functools.partial(kernel, sizes), out_shape=(jax.ShapeDtyp...  73.8 us
    unnamed x4, local copies, waits for them, and re-layouts  2.22 us

profile of v2, /device:TPU:1, one launch (start us, length us, event | category | flops | bytes accessed | tf_op | source)
XLA Modules:
  0.0 76.6 jit_solution(677678208018474126)
XLA Ops:
  0.6 73.8 %shard_map.59 = (f32[24,16,128]{2,1,0:T(8,128)}, f32[16,24]{1,0:T(8,128)}) custom-call(f32[24,16,128]{2,1,0:T(8,128)} %bitcast.16, f32[72,16,8]{2,1,0:T(8,128)} %bitcast.12, f32[24,4,2,2,192]{4,3,2,1,0:T(2,128)} %bitcast.13, f32[480,24]{1,0:T(8,128)} %bitcast.14), custom_call_target="tpu_custom_call" | custom-call | tf_op jit(solution)/shard_map/pallas_call | solution.py:721
  74.4 0.0 copy-start
  74.4 1.6 %copy.8 = f32[2,4,3,4,2,2,128]{6,5,4,3,2,1,0:T(2,128)} copy(f32[2,4,3,4,2,2,128]{6,5,4,3,2,1,0:T(2,128)} %bitcast.15) | data formatting | bytes 393216
  76.0 0.0 copy-done
  76.0 0.6 copy.9
Async XLA Ops:
  74.4 1.6 %copy-start = (f32[16,24]{1,0:T(8,128)S(1)}, f32[16,24]{1,0:T(8,128)}, u32[]{:S(2)}) copy-start(f32[16,24]{1,0:T(8,128)} %get-tuple-element.5) | copy-start | bytes 4612

commit v3 on v2

--- a/solution.py
+++ b/solution.py
@@ -122,6 +122,13 @@
     return jnp.dot(ones, low, preferred_element_type=F32) + jnp.dot(ones, high, preferred_element_type=F32)
 
 
+def rows_times(a, weights):
+    high = a.astype(jnp.bfloat16).astype(F32)
+    both = jnp.concatenate([high, a - high], axis=0).astype(jnp.bfloat16)
+    out = jnp.dot(both, weights[1], preferred_element_type=F32) + jnp.dot(both, weights[0], preferred_element_type=F32)
+    return out[0:8] + out[8:16]
+
+
 def iota(shape, dim):
     return lax.broadcasted_iota(jnp.int32, shape, dim)
 
@@ -151,7 +158,7 @@
 
 def kernel(sizes, src_in, gauge_in, null_in, coarse_in, u_out, e_out, src, gauge, null, coarse, p, u, fields, acc, links, g8,
            hx, qx, hz, qz, ht, qt, sendx, sendz, sendt, recvx, recvz, recvt, nv, nvs, nvt, low, ff, fb, wide, rows24, wrecv,
-           twice, basis, crecv, ar_send, ar_recv, isem, fsend, frecv, lsend, lrecv, wsend, wrsem, csend, crsem, asend, arsem):
+           twice, wides, twices, basis, crecv, ar_send, ar_recv, isem, fsend, frecv, lsend, lrecv, wsend, wrsem, csend, crsem, asend, arsem):
     keys, far = reach(sizes)
     me = {axis: lax.axis_index(axis) for axis in ("grp", "ta", "gz")}
     plane = sizes["grp"] * sizes["gz"]
@@ -164,7 +171,7 @@
         other = lax.rem(spot + by, plane)
         return {"grp": lax.div(other, sizes["gz"]), "gz": lax.rem(other, sizes["gz"])}
 
-    groups = ([{"ta": moved("ta", by)} for by in range(1, sizes["ta"])], [in_plane(by) for by in range(1, plane)])
+    groups = ([in_plane(by) for by in range(1, plane)], [{"ta": moved("ta", by)} for by in range(1, sizes["ta"])])
 
     def at(disp):
         return {axis: moved(axis, by) for by, (_, axis) in zip(disp, AXES)}
@@ -289,6 +296,8 @@
         for block, rows in enumerate(order):
             wide[64 * block:64 * block + 64, :] = rows
             rows24[block] = rows[0:24]
+            for part, value in enumerate(halves(rows)):
+                wides[part, 64 * block:64 * block + 64, :] = value
 
     def row_copy(block, chunk):
         first, last = CHUNKS[chunk]
@@ -326,6 +335,8 @@
                 base = 64 * keys.index(key)
                 for ri, part in ((0, product), (1, turned)):
                     twice[base + 32 * ri:base + 32 * ri + 24, :] += part[24 * other:24 * other + 24]
+        for part, value in enumerate(halves(twice[...])):
+            twices[part] = value
 
     even = (iota((3, 8, 128), 1) & 1) == 0
 
@@ -543,13 +554,13 @@
     def take_basis(step):
         for copy in coarse_copies(step):
             copy.wait()
-        once = own_y(dot(gathered(step, STENCIL), wide[...]))
+        once = own_y(rows_times(gathered(step, STENCIL), (wides[0], wides[1])))
         shifted = across(basis[2 * step])
         basis[2 * step + 1] = once + shifted
         return 2.0 * once + shifted
 
     def take_second(step, first):
-        again = own_y(dot(gathered(step, keys), twice[...]))
+        again = own_y(rows_times(gathered(step, keys), (twices[0], twices[1])))
         basis[2 * step + 2] = again + across(first)
 
     send_basis(0)
@@ -569,10 +580,7 @@
     end(0)
     begin(5)
     end(4)
-    first = take_basis(1)
-    prolong(3)
-    begin(3)
-    take_second(1, first)
+    take_second(1, take_basis(1))
 
     size = CITERS + 1
     vectors = [basis[i] for i in range(size)]
@@ -607,8 +615,6 @@
             parts = [parts[i] + parts[i + 1] if i + 1 < len(parts) else parts[i] for i in range(0, len(parts), 2)]
         return parts[0]
 
-    send_sums(0, sums)
-
     def turn(f, carry):
         end(f)
         begin(5 + f)
@@ -618,13 +624,15 @@
         end(f)
         return carry
 
+    send_sums(0, sums)
+    prolong(3)
+    begin(3)
     lax.fori_loop(1, 3, turn, 0)
-    end(5)
     send_sums(1, take_sums(0))
     end(3)
     begin(8)
-    lax.fori_loop(6, 8, settle, 0)
-    end(8)
+    end(5)
+    lax.fori_loop(6, 9, settle, 0)
     sums = take_sums(1)
 
     moments = [[None] * size for _ in range(size)]
@@ -702,8 +710,12 @@
             u_out[:, 4 * x + 2 * t:4 * x + 2 * t + 2, :] = u[:, :, :, t, 2 * x:2 * x + 2, :].reshape(24, 2, 128)
 
 
+def pinned(x):
+    return pltpu.with_memory_space_constraint(x, pltpu.HBM)
+
+
 def body(sizes, source_field, gauge_links, null_vectors, coarse_links):
-    hbm = pl.BlockSpec(memory_space=pl.ANY)
+    hbm = pl.BlockSpec(memory_space=pltpu.HBM)
     vmem = pl.BlockSpec(memory_space=pltpu.VMEM)
     keys, far = reach(sizes)
     most_rows = 64 * (len(keys) + len(keys) % 2)
@@ -716,22 +728,23 @@
                           (10, 2, 6, 8, 128), (10, 2, 2, 2, 3, 8, 128), (10, 2, 2, 2, 3, 8, 128),
                           (11, 2, 6, 8, 128), (11, 2, 2, 2, 3, 8, 128), (11, 2, 2, 2, 3, 8, 128),
                           (24, 2, 8, 192), (2, 384, 192), (2, 384, 192), (3, 96, 24), (128, 384), (256, 128), (512, 128), (8, 24, 128), (6, 8, 24, 128),
-                          (most_rows, 128), (CITERS + 1, 8, 128), (2, len(far), 8, 128), (2, 8, 128), (2, most, 8, 128)]
+                          (most_rows, 128), (2, 512, 128), (2, most_rows, 128), (CITERS + 1, 8, 128), (2, len(far), 8, 128), (2, 8, 128), (2, most, 8, 128)]
+    split = ((2, 384, 192), (2, 512, 128), (2, most_rows, 128))
     sems = [(4,), (10, 6), (11, 6), (3,), (3,), (6, 2), (6, 2), (2, len(far)), (2, len(far)), (2, most), (2, most)]
     out, found = pl.pallas_call(
         functools.partial(kernel, sizes),
         out_shape=(jax.ShapeDtypeStruct((24, 16, 128), F32), jax.ShapeDtypeStruct((16, 24), F32)),
         in_specs=[hbm] * 4,
         out_specs=(vmem, vmem),
-        scratch_shapes=[pltpu.VMEM(shape, jnp.bfloat16 if shape == (2, 384, 192) else F32) for shape in shapes]
+        scratch_shapes=[pltpu.VMEM(shape, jnp.bfloat16 if shape in split else F32) for shape in shapes]
         + [pltpu.SemaphoreType.DMA(shape) for shape in sems],
         compiler_params=pltpu.CompilerParams(
-            collective_id=0, has_side_effects=True, vmem_limit_bytes=56 * 1024 * 1024),
+            collective_id=0, has_side_effects=True, vmem_limit_bytes=32 * 1024 * 1024),
     )(
-        source_field.reshape(arguments[0]),
-        gauge_links.reshape(arguments[1]),
-        null_vectors.reshape(arguments[2]),
-        coarse_links.transpose(0, 1, 2, 4, 5, 6, 7, 3).reshape(arguments[3]),
+        pinned(source_field.reshape(arguments[0])),
+        pinned(gauge_links.reshape(arguments[1])),
+        pinned(null_vectors.reshape(arguments[2])),
+        pinned(coarse_links.transpose(0, 1, 2, 4, 5, 6, 7, 3).reshape(arguments[3])),
     )
     found = found.reshape(2, 4, 2, 24).transpose(0, 3, 1, 2)
     return out.reshape(source_field.shape), found.reshape(2, 24, 4, 1, 1, 1, 2)

time: 76.8 us -> 74.1 us (0.965)
  Pallas kernels: 73.8 us -> 72.1 us
  local copies, waits for them, and re-layouts: 2.22 us -> 1.28 us
    pallas_call x1, Pallas kernels: 73.8 us -> 72.1 us  [body(): pl.pallas_call(functools.partial(kernel, sizes), out_shape=(jax.ShapeDtyp...]
    unnamed x4 -> x2, local copies, waits for them, and re-layouts: 2.22 us -> 1.28 us
where the time goes in v3:
time: 74.1 us; the launch traced here: 74 us
  Pallas kernels  72.1 us (97%)
  local copies, waits for them, and re-layouts  1.28 us (2%)
    pallas_call x1, Pallas kernels, body(): pl.pallas_call(functools.partial(kernel, sizes), out_shape=(jax.ShapeDtyp...  72.1 us

profile of v3, /device:TPU:1, one launch (start us, length us, event | category | flops | bytes accessed | tf_op | source)
XLA Modules:
  0.0 74.0 jit_solution(11219786429701541856)
XLA Ops:
  0.6 72.1 %shard_map.59 = (f32[24,16,128]{2,1,0:T(8,128)S(1)}, f32[16,24]{1,0:T(8,128)S(1)}) custom-call(f32[24,16,128]{2,1,0:T(8,128)} %bitcast.17, f32[72,16,8]{2,1,0:T(8,128)} %bitcast.14, f32[24,4,2,2,192]{4,3,2,1,0:T(2,128)} %bitcast.15, f32[480,24]{1,0:T(8,128)} %bitcast.16), custom_call_target="tpu_custom_call" | custom-call | tf_op jit(solution)/shard_map/pallas_call | solution.py:734
  72.7 0.7 copy.8
  73.4 0.6 copy.9

commit v4 on v3

--- a/solution.py
+++ b/solution.py
@@ -234,6 +234,8 @@
                 ref[ri, s, :, t] = total[ri][s]
 
     def build_null():
+        for d in range(3):
+            low_copy(d).start()
         loads[3].wait()
         for t in range(2):
             for x in range(4):
@@ -312,8 +314,11 @@
 
         return send
 
+    def build_coarse_and_send():
+        build_coarse()
+        send_rows(0)()
+
     def build_null_and_send():
-        send_rows(0)()
         build_null_transposed()
 
     def build_twice():
@@ -327,7 +332,7 @@
             upper, lower = jnp.where(left, mine, 0.0), jnp.where(left, 0.0, mine)
             weights = jnp.concatenate([lower, upper] if flip else [upper, lower], axis=0)
             theirs = rows24[...] if block < 2 else wrecv[block - 2]
-            product = dot(theirs.reshape(8 * 24, 128), weights)
+            product = dot_halves(halves(theirs.reshape(8 * 24, 128)), halves(weights))
             real_lane = (iota((8 * 24, 128), 1) & 32) == 0
             turned = jnp.where(real_lane, -pltpu.roll(product, 96, 1), pltpu.roll(product, 32, 1))
             for other, (further, again) in enumerate(STENCIL):
@@ -479,15 +484,13 @@
         finish(0, slot, advance(k))
 
     def first_half(k, carry):
-        round_of(k, ((0, build_null), (1, build_coarse), (2, build_null_and_send), (3, send_rows(1))))
+        round_of(k, ((0, build_null), (1, build_null_and_send), (2, build_coarse_and_send), (3, send_rows(1))))
         return carry
 
     def second_half(k, carry):
         round_of(k, ())
         return carry
 
-    for d in range(3):
-        low_copy(d).start()
     lax.fori_loop(0, DEG, first_half, 0)
 
     diagonal = (iota((192, 256), 0) & 7) == (iota((192, 256), 1) & 7)
@@ -579,7 +582,6 @@
     lax.fori_loop(1, 3, lift, 0)
     end(0)
     begin(5)
-    end(4)
     take_second(1, take_basis(1))
 
     size = CITERS + 1
@@ -593,7 +595,7 @@
     products = jnp.stack(products + [none] * (32 - len(products)))
     rows = jnp.sum(jnp.where(low_half[None], products, 0.0), axis=1)
     padded = jnp.concatenate([rows, jnp.zeros((96, 128), F32)], axis=0)
-    sums = dot(jnp.ones((8, 128), F32), padded, ((1,), (1,)))
+    sums = dot(jnp.ones((8, 128), F32), padded, ((1,), (1,)))[0:1]
 
     def sum_copies(phase):
         return [pltpu.make_async_remote_copy(
@@ -631,6 +633,7 @@
     send_sums(1, take_sums(0))
     end(3)
     begin(8)
+    end(4)
     end(5)
     lax.fori_loop(6, 9, settle, 0)
     sums = take_sums(1)
@@ -728,7 +731,7 @@
                           (10, 2, 6, 8, 128), (10, 2, 2, 2, 3, 8, 128), (10, 2, 2, 2, 3, 8, 128),
                           (11, 2, 6, 8, 128), (11, 2, 2, 2, 3, 8, 128), (11, 2, 2, 2, 3, 8, 128),
                           (24, 2, 8, 192), (2, 384, 192), (2, 384, 192), (3, 96, 24), (128, 384), (256, 128), (512, 128), (8, 24, 128), (6, 8, 24, 128),
-                          (most_rows, 128), (2, 512, 128), (2, most_rows, 128), (CITERS + 1, 8, 128), (2, len(far), 8, 128), (2, 8, 128), (2, most, 8, 128)]
+                          (most_rows, 128), (2, 512, 128), (2, most_rows, 128), (CITERS + 1, 8, 128), (2, len(far), 8, 128), (2, 1, 128), (2, most, 1, 128)]
     split = ((2, 384, 192), (2, 512, 128), (2, most_rows, 128))
     sems = [(4,), (10, 6), (11, 6), (3,), (3,), (6, 2), (6, 2), (2, len(far)), (2, len(far)), (2, most), (2, most)]
     out, found = pl.pallas_call(

time: 74.1 us -> 71.9 us (0.970)
  Pallas kernels: 72.1 us -> 69.9 us
    pallas_call x1, Pallas kernels: 72.1 us -> 69.9 us  [body(): pl.pallas_call(functools.partial(kernel, sizes), out_shape=(jax.ShapeDtyp...]
where the time goes in v4:
time: 71.9 us; the launch traced here: 71.8 us
  Pallas kernels  69.9 us (97%)
  local copies, waits for them, and re-layouts  1.28 us (2%)
    pallas_call x1, Pallas kernels, body(): pl.pallas_call(functools.partial(kernel, sizes), out_shape=(jax.ShapeDtyp...  69.9 us

profile of v4, /device:TPU:1, one launch (start us, length us, event | category | flops | bytes accessed | tf_op | source)
XLA Modules:
  0.0 71.8 jit_solution(3882461499036765333)
XLA Ops:
  0.6 69.9 %shard_map.59 = (f32[24,16,128]{2,1,0:T(8,128)S(1)}, f32[16,24]{1,0:T(8,128)S(1)}) custom-call(f32[24,16,128]{2,1,0:T(8,128)} %bitcast.17, f32[72,16,8]{2,1,0:T(8,128)} %bitcast.14, f32[24,4,2,2,192]{4,3,2,1,0:T(2,128)} %bitcast.15, f32[480,24]{1,0:T(8,128)} %bitcast.16), custom_call_target="tpu_custom_call" | custom-call | tf_op jit(solution)/shard_map/pallas_call | solution.py:737
  70.5 0.7 copy.8
  71.2 0.6 copy.9

commit v5 on v4

--- a/solution.py
+++ b/solution.py
@@ -487,10 +487,6 @@
         round_of(k, ((0, build_null), (1, build_null_and_send), (2, build_coarse_and_send), (3, send_rows(1))))
         return carry
 
-    def second_half(k, carry):
-        round_of(k, ())
-        return carry
-
     lax.fori_loop(0, DEG, first_half, 0)
 
     diagonal = (iota((192, 256), 0) & 7) == (iota((192, 256), 1) & 7)
@@ -697,20 +693,31 @@
                 p[ri, s, :, t] = after
                 u[ri, s, :, t] = result + step + after
 
-    found = none
-    for i in range(CITERS):
-        found = found + (answer[i][0] * vectors[i] - answer[i][1] * turned[i])
-    for ri in range(2):
-        part = found if ri == 0 else pltpu.roll(found, 96, 1)
-        for c in range(4):
-            for y in range(2):
-                at = 8 * ri + 2 * c + y
-                e_out[at:at + 1, :] = part[4 * y + c:4 * y + c + 1, 0:24]
-
-    lax.fori_loop(DEG + 2, 2 * DEG, second_half, 0)
-    for t in range(2):
-        for x in range(4):
-            u_out[:, 4 * x + 2 * t:4 * x + 2 * t + 2, :] = u[:, :, :, t, 2 * x:2 * x + 2, :].reshape(24, 2, 128)
+    def write_found():
+        found = none
+        for i in range(CITERS):
+            found = found + (answer[i][0] * vectors[i] - answer[i][1] * turned[i])
+        for ri in range(2):
+            part = found if ri == 0 else pltpu.roll(found, 96, 1)
+            for c in range(4):
+                for y in range(2):
+                    row = 8 * ri + 2 * c + y
+                    e_out[row:row + 1, :] = part[4 * y + c:4 * y + c + 1, 0:24]
+
+    def last(t, total):
+        for ri in range(2):
+            for s in range(4):
+                step = ALPHA[-1] * p[ri, s, :, t] + BETA[-1] * (r[ri, s, :, t] - total[ri][s])
+                value = u[ri, s, :, t] + step
+                at = 12 * ri + 3 * s
+                for x in range(4):
+                    u_out[at:at + 3, 4 * x + 2 * t:4 * x + 2 * t + 2, :] = value[:, 2 * x:2 * x + 2]
+
+    start(p, 0, 0)
+    write_found()
+    finish(0, 0, advance(2 * DEG - 2))
+    start(p, 0, 1)
+    finish(0, 1, last)
 
 
 def pinned(x):

time: 71.9 us -> 71.8 us (level)
  no operation moved by 1% of the time
where the time goes in v5:
time: 71.8 us; the launch traced here: 71.7 us
  Pallas kernels  69.8 us (97%)
  local copies, waits for them, and re-layouts  1.28 us (2%)
    pallas_call x1, Pallas kernels, body(): pl.pallas_call(functools.partial(kernel, sizes), out_shape=(jax.ShapeDtyp...  69.8 us

profile of v5, /device:TPU:1, one launch (start us, length us, event | category | flops | bytes accessed | tf_op | source)
XLA Modules:
  0.0 71.7 jit_solution(16397859878356033417)
XLA Ops:
  0.6 69.8 %shard_map.59 = (f32[24,16,128]{2,1,0:T(8,128)S(1)}, f32[16,24]{1,0:T(8,128)S(1)}) custom-call(f32[24,16,128]{2,1,0:T(8,128)} %bitcast.17, f32[72,16,8]{2,1,0:T(8,128)} %bitcast.14, f32[24,4,2,2,192]{4,3,2,1,0:T(2,128)} %bitcast.15, f32[480,24]{1,0:T(8,128)} %bitcast.16), custom_call_target="tpu_custom_call" | custom-call | tf_op jit(solution)/shard_map/pallas_call | solution.py:744
  70.4 0.7 copy.8
  71.1 0.6 copy.9
